TPU v7x, 32 devices: a whole 2x2x4 slice. The times are simulated.
32 devices in a mesh: row: 8 (over y, x, core), col: 4 (over z).
Axes of the slice: x: 2, y: 2, z: 4, core: 2. Of those that a mesh axis runs over, the one named last changes fastest.
Arguments:
- latents: bfloat16 [512, 6144], P('col', 'row'), may hold values from -6 to 6
- w_in: bfloat16 [6144, 24576], P('row', 'col'), may hold values from -0.078125 to 0.078125
- w_out: bfloat16 [24576, 6144], P('col', 'row'), may hold values from -0.0390625 to 0.0390625
- cotangent: bfloat16 [512, 6144], P('col', 'row'), may hold values from -0.625 to 0.625
Outputs:
- mixed: bfloat16 [512, 6144], P('col', 'row')
- grad_w_in: bfloat16 [6144, 24576], P('row', 'col')
- grad_w_out: bfloat16 [24576, 6144], P('col', 'row')
All inputs are finite; a program needn't handle non-finite values.
Results may differ from a plain program's by a relative error of at most 0.03.
Values may be sent and summed in bfloat16 or wider, within the bound.
No kernel may reach another device: no remote copies, remote signals or barrier semaphores. Data moves between devices by JAX's collectives and lax.ppermute only.
A program may use at most 128 MiB of HBM per device.

v0:
```python
import jax
import jax.numpy as jnp
from jax import lax
from jax.sharding import PartitionSpec as P

f32 = jnp.float32
bf16 = jnp.bfloat16


def gelu_parts(hidden):
    cdf = 0.5 * (1.0 + jax.scipy.special.erf(hidden * 0.7071067811865476))
    pdf = jnp.exp(-0.5 * hidden * hidden) * 0.3989422804014327
    return (hidden * cdf, cdf + hidden * pdf)


def weight_grad(piece, rows, half, p, into, across):
    quarter = piece.shape[1]
    at = (half * 2 + p) * quarter
    if across:
        out = jnp.dot(rows, piece, preferred_element_type=f32).astype(bf16)
        return lax.dynamic_update_slice(into, out, (0, at))
    out = lax.dot_general(piece, rows, (((0,), (0,)), ((), ())), preferred_element_type=f32).astype(bf16)
    return lax.dynamic_update_slice(into, out, (at, 0))


def down(piece, w_out, half, p, add):
    quarter = piece.shape[1]
    block = lax.dynamic_slice_in_dim(w_out, (half * 2 + p) * quarter, quarter, 0)
    out = jnp.dot(piece, block, preferred_element_type=f32)
    return out if add is None else add + out


def make(n_row, n_col):
    row_bits = n_row.bit_length() - 1
    first = tuple(range(1, row_bits))
    orders = (first, first[::-1])
    steps = len(first)

    def swap_core(v):
        return lax.ppermute(v, "row", [(i, i ^ 1) for i in range(n_row)])

    def swap_chip(v, step):
        return lax.ppermute(v, "row", [(i, i ^ (1 << orders[i & 1][step])) for i in range(n_row)])

    def part(v, axis, index):
        return lax.slice_in_dim(v, index, index + 1, axis=axis)

    def flips(v, order, axis):
        me = lax.axis_index("row")
        for k, bit in enumerate(order):
            v = jnp.where((me >> bit) & 1 == 1, jnp.flip(v, axis + k), v)
        return v

    def relative(v):
        v = v.reshape((2,) * steps + (1, v.shape[0] >> steps, v.shape[1]))
        return flips(v, first, 0)

    def turn(v):
        return v.transpose(tuple(range(steps))[::-1] + tuple(range(steps, v.ndim)))

    def after(v, *tokens):
        return lax.optimization_barrier((v,) + tokens)[0]

    def flat(v):
        return v.reshape(-1, v.shape[-1])

    def scatter(parts, *tokens):
        core = lax.axis_index("row") & 1
        second = turn(parts[1])
        got = swap_core(jnp.where(core == 0, second, parts[0]))
        v = jnp.where(core == 0, parts[0], second)
        v = (v.astype(f32) + after(got, *tokens).astype(f32)).astype(bf16)
        seen = [v]
        for k in range(steps):
            got = swap_chip(part(v, k, 1), k)
            seen.append(got)
            v = part(v, k, 0).astype(f32) + got.astype(f32)
            if k + 1 < steps:
                v = v.astype(bf16)
        return v, seen

    def gather_chips(v, stop):
        for k in reversed(range(stop, steps)):
            v = lax.concatenate([v, swap_chip(v, k)], k)
        return v

    def per_device(latents, w_in, w_out, cotangent):
        tokens, width = latents.shape
        cut = w_in.shape[1] // 2
        core = lax.axis_index("row") & 1
        halves = [slice(h * cut, (h + 1) * cut) for h in (0, 1)]
        own_half = core.astype(jnp.int32)
        other_half = 1 - own_half

        def up(x):
            out = [jnp.dot(flat(x), w_in[:, h], preferred_element_type=f32) for h in halves]
            return [v.astype(bf16).reshape(x.shape[:-1] + (cut,)) for v in out]

        def back(c):
            out = [
                lax.dot_general(flat(c), w_out[h], (((1,), (1,)), ((), ())), preferred_element_type=f32)
                for h in halves
            ]
            return [v.astype(bf16).reshape(c.shape[:-1] + (cut,)) for v in out]

        def both(x, c, *tokens):
            n = x.shape[steps]
            v, seen = scatter([lax.concatenate(pair, steps) for pair in zip(up(x), back(c))], *tokens)
            hid = lax.slice_in_dim(v, 0, n, axis=steps)
            grad = lax.slice_in_dim(v, n, 2 * n, axis=steps)
            return hid, grad, seen

        mine = lax.optimization_barrier(lax.concatenate([relative(latents), relative(cotangent)], steps + 2))
        every = lax.all_gather(mine, "col", axis=steps, tiled=True)

        def rolled(v, by):
            n = v.shape[steps]
            return lax.dynamic_slice_in_dim(lax.concatenate([v, v], steps), by, n, steps)

        here = lax.axis_index("col")
        x_own, c_own = mine[..., :width], mine[..., width:]
        others = lax.slice_in_dim(rolled(every, here), 1, n_col, axis=steps)
        x_others, c_others = others[..., :width], others[..., width:]
        x_all = lax.concatenate([x_own, x_others], steps)
        c_all = lax.concatenate([c_own, c_others], steps)

        hid, grad, seen = both(x_own, c_own)
        hid_others, seen_hid = scatter(up(after(x_others, seen[1])))
        grad_others, seen_grad = scatter(back(after(c_others, seen_hid[0])))
        hids, grads = [hid, hid_others], [grad, grad_others]

        hid = lax.concatenate(hids, steps)
        act = gelu_parts(hid)[0].astype(bf16)
        grad = lax.concatenate(grads, steps)
        hid, grad = lax.optimization_barrier((hid, grad))
        grad = (grad * gelu_parts(hid)[1]).astype(bf16)

        quarter = cut // 2

        def gather(v, p):
            w = v[..., p * quarter : (p + 1) * quarter]
            return lax.concatenate([w, swap_chip(w, 0)], 0)

        x_turned, c_turned = turn(x_all), turn(c_all)

        def ordered(plain, turned, half):
            return jnp.where(half == 0, flat(plain), flat(turned))

        x_rows = [lax.optimization_barrier(ordered(x_all, x_turned, h).T) for h in (own_half, other_half)]
        c_rows = [lax.optimization_barrier(ordered(c_all, c_turned, h)) for h in (own_half, other_half)]

        act = gather_chips(act, 1)
        grad = gather_chips(grad, 1)
        sums = [None, None]
        grad_w_out = jnp.zeros_like(w_out)
        grad_w_in = jnp.zeros_like(w_in)
        acts = [gather(act, p) for p in range(2)]
        grads = [gather(grad, p) for p in range(2)]
        for p in range(2):
            pieces = (acts[p], swap_core(acts[p]))
            for i, half in enumerate((own_half, other_half)):
                sums[i] = down(flat(pieces[i]), w_out, half, p, sums[i])
                grad_w_out = weight_grad(flat(pieces[i]), c_rows[i], half, p, grad_w_out, False)
        grads[1] = after(grads[1], grad_w_out)
        for p in range(2):
            pieces = (grads[p], swap_core(grads[p]))
            for i, half in enumerate((own_half, other_half)):
                grad_w_in = weight_grad(flat(pieces[i]), x_rows[i], half, p, grad_w_in, True)

        sums = [v.reshape(x_all.shape) for v in sums]
        mixed = jnp.where(core == 0, sums[0], sums[1]) + turn(jnp.where(core == 0, sums[1], sums[0]))
        mixed = mixed.astype(bf16)
        mixed = rolled(mixed, (n_col - here) % n_col)
        mixed = lax.psum_scatter(mixed, "col", scatter_dimension=steps, tiled=True)
        mixed = flips(mixed, first, 0).reshape(tokens, width)
        return (mixed, grad_w_in, grad_w_out)

    return per_device


def solution(mesh):
    placed = (P("col", "row"), P("row", "col"), P("col", "row"), P("col", "row"))
    return jax.shard_map(
        make(mesh.shape["row"], mesh.shape["col"]),
        mesh=mesh,
        in_specs=placed,
        out_specs=(P("col", "row"), P("row", "col"), P("col", "row")),
        check_vma=False,
    )
```

profile of v0, /device:TPU:0, one launch (start us, length us, event | category | flops | bytes accessed | tf_op | source)
XLA Modules:
  0.0 241.0 jit_solution(11050424561778410058)
XLA Ops:
  9.5 4.1 %fusion.21 = bf16[128,3072]{1,0:T(8,128)(2,1)S(1)} fusion(bf16[128,768]{1,0:T(8,128)(2,1)S(1)} %bitcast.136, bf16[6144,768]{1,0:T(8,128)(2,1)} %param.6), kind=kOutput, calls=%fused_computation.21 | convolution fusion | flops 604372992 | bytes 5701632 | tf_op jit(solution)/shard_map/dot_general | solution.py:101
  13.7 4.0 %fusion.15 = bf16[128,3072]{1,0:T(8,128)(2,1)S(1)} fusion(bf16[128,768]{1,0:T(8,128)(2,1)S(1)} %bitcast.137, bf16[6144,768]{1,0:T(8,128)(2,1)} %param.6), kind=kOutput, calls=%fused_computation.19 | convolution fusion | flops 604372992 | bytes 5701632 | tf_op jit(solution)/shard_map/dot_general | solution.py:101
  21.8 3.1 %collective-permute-done = bf16[2,2,2,32,3072]{4,3,1,0,2:T(8,128)(2,1)} collective-permute-done((bf16[2,2,2,32,3072]{4,3,1,0,2:T(8,128)(2,1)}, bf16[2,2,2,32,3072]{4,3,1,0,2:T(8,128)(2,1)}, u32[]{:S(2)}, u32[]{:S(2)}) %collective-permute-start) | collective-permute-done | bytes 1572896 | tf_op jit(solution)/shard_map/ppermute | solution.py:40
  24.9 2.6 %add_convert_fusion.2 = bf16[2,2,2,32,3072]{4,3,1,0,2:T(8,128)(2,1)S(1)} fusion(bf16[2,2,2,32,3072]{4,3,1,0,2:T(8,128)(2,1)} %collective-permute-done, pred[]{:T(512)S(6)} %eq.11, bf16[2,2,1,32,3072]{4,3,1,0,2:T(8,128)(2,1)S(1)} %bitcast.107, bf16[2,2,1,32,3072]{4,3,1,0,2:T(8,128)(2,1)} %bitcast.111, bf16[2,2,1,32,3072]{4,3,1,0,2:T(8,128)(2,1)S(1)} %bitcast.105, ...), kind=kLoop, calls=%fused_computation.40 | loop fusion | flops 7864320 | bytes 6291457 | tf_op jit(solution)/shard_map/convert_element_type | solution.py:72
  27.6 2.9 %collective-permute-start.1 = (bf16[1,2,2,32,3072]{4,3,1,0,2:T(8,128)(2,1)S(1)}, bf16[1,2,2,32,3072]{4,3,1,0,2:T(8,128)(2,1)}, u32[]{:S(2)}, u32[]{:S(2)}) collective-permute-start(bf16[1,2,2,32,3072]{4,3,1,0,2:T(8,128)(2,1)S(1)} %slice.114), channel_id=1, source_target_pairs={{0,8},{4,20},{8,0},{12,28},{16,24},{20,4},{24,16},{28,12},{1,9},{5... | collective-permute-start | bytes 2359304 | tf_op jit(solution)/shard_map/ppermute | solution.py:43
  30.5 30.7 %all-gather.2.cloned.1.call-done = bf16[2,2,4,32,1536]{4,3,1,0,2:T(8,128)(2,1)} async-done(((bf16[2,2,1,32,1536]{4,3,1,0,2:T(8,128)(2,1)}), bf16[2,2,4,32,1536]{4,3,1,0,2:T(8,128)(2,1)}) %all-gather.2.cloned.1.call-update) | async-done | bytes 1572880 | tf_op jit(solution)/shard_map/all_gather | solution.py:114
  63.4 4.3 %convolution_convert_fusion.2 = bf16[384,3072]{1,0:T(8,128)(2,1)S(1)} fusion(bf16[384,768]{1,0:T(8,128)(2,1)S(1)} %bitcast.128, bf16[768,6144]{1,0:T(8,128)(2,1)} %param.5), kind=kOutput, calls=%fused_computation.4 | convolution fusion | flops 1813118976 | bytes 7667712 | tf_op jit(solution)/shard_map/dot_general | solution.py:96
  67.7 4.3 %convolution_convert_fusion.3 = bf16[384,3072]{1,0:T(8,128)(2,1)S(1)} fusion(bf16[384,768]{1,0:T(8,128)(2,1)S(1)} %bitcast.129, bf16[768,6144]{1,0:T(8,128)(2,1)} %param.5), kind=kOutput, calls=%fused_computation.5 | convolution fusion | flops 1813118976 | bytes 7667712 | tf_op jit(solution)/shard_map/dot_general | solution.py:96
  84.4 14.3 %collective-permute-done.4 = bf16[1,2,3,32,3072]{4,3,2,1,0:T(8,128)(2,1)S(1)} collective-permute-done((bf16[1,2,3,32,3072]{4,3,2,1,0:T(8,128)(2,1)S(1)}, bf16[1,2,3,32,3072]{4,3,2,1,0:T(8,128)(2,1)S(1)}, u32[]{:S(2)}, u32[]{:S(2)}) %collective-permute-start.4) | collective-permute-done | bytes 1179680 | tf_op jit(solution)/shard_map/ppermute | solution.py:43
  101.5 7.6 %collective-permute-done.5 = bf16[1,1,3,32,3072]{4,3,2,1,0:T(8,128)(2,1)S(1)} collective-permute-done((bf16[1,1,3,32,3072]{4,3,2,1,0:T(8,128)(2,1)S(1)}, bf16[1,1,3,32,3072]{4,3,2,1,0:T(8,128)(2,1)S(1)}, u32[]{:S(2)}, u32[]{:S(2)}) %collective-permute-start.5) | collective-permute-done | bytes 589856 | tf_op jit(solution)/shard_map/ppermute | solution.py:43
  118.5 15.8 %collective-permute-done.6 = bf16[1,1,4,32,3072]{4,3,2,1,0:T(8,128)(2,1)} collective-permute-done((bf16[1,1,4,32,3072]{4,3,2,1,0:T(8,128)(2,1)}, bf16[1,1,4,32,3072]{4,3,2,1,0:T(8,128)(2,1)}, u32[]{:S(2)}, u32[]{:S(2)}) %collective-permute-start.6) | collective-permute-done | bytes 786464 | tf_op jit(solution)/shard_map/ppermute | solution.py:43
  141.2 21.4 %collective-permute-done.8 = bf16[1,2,4,32,1536]{4,3,2,1,0:T(8,128)(2,1)S(1)} collective-permute-done((bf16[1,2,4,32,1536]{4,3,2,1,0:T(8,128)(2,1)S(1)}, bf16[1,2,4,32,1536]{4,3,2,1,0:T(8,128)(2,1)S(1)}, u32[]{:S(2)}, u32[]{:S(2)}) %collective-permute-start.8) | collective-permute-done | bytes 786464 | tf_op jit(solution)/shard_map/ppermute | solution.py:43
  169.9 7.1 %fusion.36 = f32[512,768]{1,0:T(8,128)S(1)} fusion(bf16[512,1536]{1,0:T(8,128)(2,1)S(1)} %bitcast.112, bf16[6144,768]{1,0:T(8,128)(2,1)} %param.6, s32[]{:T(128)S(6)} %select_n.162), kind=kOutput, calls=%fused_computation.51 | convolution fusion | flops 1207959552 | bytes 5505028 | tf_op jit(solution)/shard_map/dot_general | solution.py:29
  181.9 2.8 %fusion.32 = f32[512,768]{1,0:T(8,128)S(1)} fusion(bf16[512,1536]{1,0:T(8,128)(2,1)} %bitcast.17, bf16[6144,768]{1,0:T(8,128)(2,1)S(1)} %bitcast.133, s32[]{:T(128)S(6)} %select_n.164), kind=kOutput, calls=%fused_computation.47 | convolution fusion | flops 1207959552 | bytes 5505028 | tf_op jit(solution)/shard_map/dot_general | solution.py:29
  187.6 4.6 %fusion.28 = bf16[6144,768]{1,0:T(8,128)(2,1)} fusion(bf16[6144,768]{1,0:T(8,128)(2,1)} %copy-done, s32[]{:T(128)S(6)} %select_n.163, bf16[512,1536]{1,0:T(8,128)(2,1)} %bitcast.117, bf16[512,768]{1,0:T(8,128)(2,1)} %bitcast.118), kind=kOutput, calls=%fused_computation.31 | convolution fusion | flops 1209139200 | bytes 4718596 | tf_op jit(solution)/shard_map/dot_general | solution.py:22
  192.2 3.1 %fusion.27 = bf16[6144,768]{1,0:T(8,128)(2,1)} fusion(bf16[6144,768]{1,0:T(8,128)(2,1)} %fusion.28, s32[]{:T(128)S(6)} %select_n.162, bf16[512,1536]{1,0:T(8,128)(2,1)S(1)} %bitcast.113, bf16[512,768]{1,0:T(8,128)(2,1)S(1)} %bitcast.121), kind=kOutput, calls=%fused_computation.29 | convolution fusion | flops 1209139200 | bytes 4718596 | tf_op jit(solution)/shard_map/dot_general | solution.py:22
  195.4 5.0 %collective-permute-done.15 = bf16[1,2,4,32,1536]{4,3,2,1,0:T(8,128)(2,1)} collective-permute-done((bf16[1,2,4,32,1536]{4,3,2,1,0:T(8,128)(2,1)S(1)}, bf16[1,2,4,32,1536]{4,3,2,1,0:T(8,128)(2,1)}, u32[]{:S(2)}, u32[]{:S(2)}) %collective-permute-start.15) | collective-permute-done | bytes 786464 | tf_op jit(solution)/shard_map/ppermute | solution.py:43
  202.8 4.3 %fusion.26 = bf16[6144,768]{1,0:T(8,128)(2,1)} fusion(bf16[6144,768]{1,0:T(8,128)(2,1)} %fusion.27, s32[]{:T(128)S(6)} %select_n.164, bf16[512,1536]{1,0:T(8,128)(2,1)} %bitcast.17, bf16[512,768]{1,0:T(8,128)(2,1)S(1)} %bitcast.119), kind=kOutput, calls=%fused_computation.27 | convolution fusion | flops 1209139200 | bytes 4718596 | tf_op jit(solution)/shard_map/dot_general | solution.py:22
  207.0 2.5 %pad_maximum_fusion.7 = bf16[2,2,4,32,1536]{4,3,2,1,0:T(8,128)(2,1)} fusion(bf16[1,2,4,32,1536]{4,3,2,1,0:T(8,128)(2,1)} %collective-permute-done.17, bf16[1,2,4,32,1536]{4,3,2,1,0:T(8,128)(2,1)S(1)} %get-tuple-element.15), kind=kLoop, calls=%fused_computation.76 | loop fusion | flops 786432 | bytes 3145728 | tf_op jit(solution)/shard_map/concatenate | solution.py:142
  210.1 4.9 %broadcast_in_dim.6 = bf16[768,6144]{1,0:T(8,128)(2,1)} broadcast(bf16[]{:T(256)} %constant.46.clone.1), dimensions={} | broadcast | bytes 9437186 | tf_op jit(solution)/shard_map/broadcast_in_dim | solution.py:156
  215.0 4.2 %fusion.31 = bf16[768,6144]{1,0:T(8,128)(2,1)} fusion(bf16[768,6144]{1,0:T(8,128)(2,1)} %broadcast_in_dim.6, s32[]{:T(128)S(6)} %select_n.161, bf16[768,512]{0,1:T(8,128)(2,1)S(1)} %bitcast.124, bf16[512,1536]{1,0:T(8,128)(2,1)} %bitcast.31), kind=kOutput, calls=%fused_computation.37 | convolution fusion | flops 1209139200 | bytes 4718596 | tf_op jit(solution)/shard_map/dot_general | solution.py:20
  221.0 4.2 %fusion.30 = bf16[768,6144]{1,0:T(8,128)(2,1)} fusion(bf16[768,6144]{1,0:T(8,128)(2,1)} %fusion.31, s32[]{:T(128)S(6)} %select_n.163, bf16[768,512]{0,1:T(8,128)(2,1)S(1)} %bitcast.122, bf16[512,1536]{1,0:T(8,128)(2,1)} %bitcast.34), kind=kOutput, calls=%fused_computation.35 | convolution fusion | flops 1209139200 | bytes 4718596 | tf_op jit(solution)/shard_map/dot_general | solution.py:20
  225.3 4.2 %fusion.25 = bf16[768,6144]{1,0:T(8,128)(2,1)} fusion(bf16[768,6144]{1,0:T(8,128)(2,1)} %fusion.30, s32[]{:T(128)S(6)} %select_n.162, bf16[768,512]{0,1:T(8,128)(2,1)S(1)} %bitcast.125, bf16[512,1536]{1,0:T(8,128)(2,1)} %bitcast.39), kind=kOutput, calls=%fused_computation.25 | convolution fusion | flops 1209139200 | bytes 4718596 | tf_op jit(solution)/shard_map/dot_general | solution.py:20
  229.5 4.2 %fusion.24 = bf16[768,6144]{1,0:T(8,128)(2,1)} fusion(bf16[768,6144]{1,0:T(8,128)(2,1)} %fusion.25, s32[]{:T(128)S(6)} %select_n.164, bf16[768,512]{0,1:T(8,128)(2,1)S(1)} %bitcast.123, bf16[512,1536]{1,0:T(8,128)(2,1)} %bitcast.40), kind=kOutput, calls=%fused_computation.23 | convolution fusion | flops 1209139200 | bytes 4718596 | tf_op jit(solution)/shard_map/dot_general | solution.py:20
  (129 shorter events, 59.5 us)
Async XLA Ops:
  7.2 54.0 %all-gather.2.cloned.1.call-start = ((), (), s32[]{:S(2)}) async-start(), calls=%async_computation.1 | async-start | bytes 1966080 | tf_op jit(solution)/shard_map/all_gather | solution.py:114
  21.1 3.8 %collective-permute-start = (bf16[2,2,2,32,3072]{4,3,1,0,2:T(8,128)(2,1)}, bf16[2,2,2,32,3072]{4,3,1,0,2:T(8,128)(2,1)}, u32[]{:S(2)}, u32[]{:S(2)}) collective-permute-start(bf16[2,2,2,32,3072]{4,3,1,0,2:T(8,128)(2,1)} %bitcast_select_fusion.4), channel_id=1, source_target_pairs={{0,4},{4,0},{8,12},{12,8},{16,20},{20,16},{24,28},{28,24},{1,5},{5... | collective-permute-start | bytes 4718600 | tf_op jit(solution)/shard_map/ppermute | solution.py:40
  21.5 197.7 %reduce-scatter.2.cloned.1.call-start = ((), (), s32[]{:S(2)}) async-start(), calls=%async_computation.2 | async-start | bytes 983040 | tf_op jit(solution)/shard_map/reduce_scatter | solution.py:174
  27.6 35.8 %collective-permute-start.1 = (bf16[1,2,2,32,3072]{4,3,1,0,2:T(8,128)(2,1)S(1)}, bf16[1,2,2,32,3072]{4,3,1,0,2:T(8,128)(2,1)}, u32[]{:S(2)}, u32[]{:S(2)}) collective-permute-start(bf16[1,2,2,32,3072]{4,3,1,0,2:T(8,128)(2,1)S(1)} %slice.114), channel_id=1, source_target_pairs={{0,8},{4,20},{8,0},{12,28},{16,24},{20,4},{24,16},{28,12},{1,9},{5... | collective-permute-start | bytes 2359304 | tf_op jit(solution)/shard_map/ppermute | solution.py:43
  72.3 4.6 %collective-permute-start.3 = (bf16[2,2,3,32,3072]{4,3,2,1,0:T(8,128)(2,1)S(1)}, bf16[2,2,3,32,3072]{4,3,2,1,0:T(8,128)(2,1)S(1)}, u32[]{:S(2)}, u32[]{:S(2)}) collective-permute-start(bf16[2,2,3,32,3072]{4,3,2,1,0:T(8,128)(2,1)S(1)} %bitcast_select_fusion.2), channel_id=1, source_target_pairs={{0,4},{4,0},{8,12},{12,8},{16,20},{20,16},{24,28},{28,24},{1,5},{5... | collective-permute-start | bytes 7077896 | tf_op jit(solution)/shard_map/ppermute | solution.py:40
  74.0 10.3 %collective-permute-start.2 = (bf16[1,1,2,32,3072]{4,3,1,0,2:T(8,128)(2,1)S(1)}, bf16[1,1,2,32,3072]{4,3,1,0,2:T(8,128)(2,1)S(1)}, u32[]{:S(2)}, u32[]{:S(2)}) collective-permute-start(bf16[1,1,2,32,3072]{4,3,1,0,2:T(8,128)(2,1)S(1)} %slice.116), channel_id=1, source_target_pairs={{0,16},{4,12},{8,24},{12,4},{16,0},{20,28},{24,8},{28,20},{1,17},{... | collective-permute-start | bytes 1179656 | tf_op jit(solution)/shard_map/ppermute | solution.py:43
  82.5 16.3 %collective-permute-start.4 = (bf16[1,2,3,32,3072]{4,3,2,1,0:T(8,128)(2,1)S(1)}, bf16[1,2,3,32,3072]{4,3,2,1,0:T(8,128)(2,1)S(1)}, u32[]{:S(2)}, u32[]{:S(2)}) collective-permute-start(bf16[1,2,3,32,3072]{4,3,2,1,0:T(8,128)(2,1)S(1)} %slice.120), channel_id=1, source_target_pairs={{0,8},{4,20},{8,0},{12,28},{16,24},{20,4},{24,16},{28,12},{1,9},{5... | collective-permute-start | bytes 3538952 | tf_op jit(solution)/shard_map/ppermute | solution.py:43
  84.2 25.0 %collective-permute-start.11 = (bf16[2,2,3,32,3072]{4,3,2,1,0:T(8,128)(2,1)S(1)}, bf16[2,2,3,32,3072]{4,3,2,1,0:T(8,128)(2,1)S(1)}, u32[]{:S(2)}, u32[]{:S(2)}) collective-permute-start(bf16[2,2,3,32,3072]{4,3,2,1,0:T(8,128)(2,1)S(1)} %bitcast_select_fusion), channel_id=1, source_target_pairs={{0,4},{4,0},{8,12},{12,8},{16,20},{20,16},{24,28},{28,24},{1,5},{5... | collective-permute-start | bytes 7077896 | tf_op jit(solution)/shard_map/ppermute | solution.py:40
  99.2 9.9 %collective-permute-start.5 = (bf16[1,1,3,32,3072]{4,3,2,1,0:T(8,128)(2,1)S(1)}, bf16[1,1,3,32,3072]{4,3,2,1,0:T(8,128)(2,1)S(1)}, u32[]{:S(2)}, u32[]{:S(2)}) collective-permute-start(bf16[1,1,3,32,3072]{4,3,2,1,0:T(8,128)(2,1)S(1)} %slice.122), channel_id=1, source_target_pairs={{0,16},{4,12},{8,24},{12,4},{16,0},{20,28},{24,8},{28,20},{1,17},{... | collective-permute-start | bytes 1769480 | tf_op jit(solution)/shard_map/ppermute | solution.py:43
  111.9 26.0 %collective-permute-start.12 = (bf16[1,2,3,32,3072]{4,3,2,1,0:T(8,128)(2,1)}, bf16[1,2,3,32,3072]{4,3,2,1,0:T(8,128)(2,1)}, u32[]{:S(2)}, u32[]{:S(2)}) collective-permute-start(bf16[1,2,3,32,3072]{4,3,2,1,0:T(8,128)(2,1)} %slice.128), channel_id=1, source_target_pairs={{0,8},{4,20},{8,0},{12,28},{16,24},{20,4},{24,16},{28,12},{1,9},{5... | collective-permute-start | bytes 3538952 | tf_op jit(solution)/shard_map/ppermute | solution.py:43
  115.1 19.2 %collective-permute-start.6 = (bf16[1,1,4,32,3072]{4,3,2,1,0:T(8,128)(2,1)}, bf16[1,1,4,32,3072]{4,3,2,1,0:T(8,128)(2,1)}, u32[]{:S(2)}, u32[]{:S(2)}) collective-permute-start(bf16[1,1,4,32,3072]{4,3,2,1,0:T(8,128)(2,1)} %get-tuple-element.20), channel_id=1, source_target_pairs={{0,16},{4,12},{8,24},{12,4},{16,0},{20,28},{24,8},{28,20},{1,17},{... | collective-permute-start | bytes 2359304 | tf_op jit(solution)/shard_map/ppermute | solution.py:43
  118.5 49.9 %copy-start.11 = (bf16[2,2,4,32,768]{4,3,2,1,0:T(8,128)(2,1)}, bf16[2,2,4,32,768]{4,3,2,1,0:T(8,128)(2,1)S(1)}, u32[]{:S(2)}) copy-start(bf16[2,2,4,32,768]{4,3,2,1,0:T(8,128)(2,1)S(1)} %get-tuple-element.24) | copy-start | bytes 2359300
  135.8 27.0 %collective-permute-start.7 = (bf16[1,2,4,32,1536]{4,3,2,1,0:T(8,128)(2,1)S(1)}, bf16[1,2,4,32,1536]{4,3,2,1,0:T(8,128)(2,1)S(1)}, u32[]{:S(2)}, u32[]{:S(2)}) collective-permute-start(bf16[1,2,4,32,1536]{4,3,2,1,0:T(8,128)(2,1)S(1)} %get-tuple-element.21), channel_id=1, source_target_pairs={{0,8},{4,20},{8,0},{12,28},{16,24},{20,4},{24,16},{28,12},{1,9},{5... | collective-permute-start | bytes 2359304 | tf_op jit(solution)/shard_map/ppermute | solution.py:43
  137.3 25.3 %collective-permute-start.8 = (bf16[1,2,4,32,1536]{4,3,2,1,0:T(8,128)(2,1)S(1)}, bf16[1,2,4,32,1536]{4,3,2,1,0:T(8,128)(2,1)S(1)}, u32[]{:S(2)}, u32[]{:S(2)}) collective-permute-start(bf16[1,2,4,32,1536]{4,3,2,1,0:T(8,128)(2,1)S(1)} %get-tuple-element.22), channel_id=1, source_target_pairs={{0,8},{4,20},{8,0},{12,28},{16,24},{20,4},{24,16},{28,12},{1,9},{5... | collective-permute-start | bytes 2359304 | tf_op jit(solution)/shard_map/ppermute | solution.py:43
  139.6 23.9 %collective-permute-start.13 = (bf16[1,1,3,32,3072]{4,3,2,1,0:T(8,128)(2,1)S(1)}, bf16[1,1,3,32,3072]{4,3,2,1,0:T(8,128)(2,1)S(1)}, u32[]{:S(2)}, u32[]{:S(2)}) collective-permute-start(bf16[1,1,3,32,3072]{4,3,2,1,0:T(8,128)(2,1)S(1)} %slice.130), channel_id=1, source_target_pairs={{0,16},{4,12},{8,24},{12,4},{16,0},{20,28},{24,8},{28,20},{1,17},{... | collective-permute-start | bytes 1769480 | tf_op jit(solution)/shard_map/ppermute | solution.py:43
  162.7 19.1 %collective-permute-start.10 = (bf16[2,2,4,32,1536]{4,3,2,1,0:T(8,128)(2,1)S(1)}, bf16[2,2,4,32,1536]{4,3,2,1,0:T(8,128)(2,1)}, u32[]{:S(2)}, u32[]{:S(2)}) collective-permute-start(bf16[2,2,4,32,1536]{4,3,2,1,0:T(8,128)(2,1)S(1)} %pad_maximum_fusion.4), channel_id=1, source_target_pairs={{0,4},{4,0},{8,12},{12,8},{16,20},{20,16},{24,28},{28,24},{1,5},{5... | collective-permute-start | bytes 4718600 | tf_op jit(solution)/shard_map/ppermute | solution.py:40
  163.0 21.7 %collective-permute-start.9 = (bf16[2,2,4,32,1536]{4,3,2,1,0:T(8,128)(2,1)S(1)}, bf16[2,2,4,32,1536]{4,3,2,1,0:T(8,128)(2,1)S(1)}, u32[]{:S(2)}, u32[]{:S(2)}) collective-permute-start(bf16[2,2,4,32,1536]{4,3,2,1,0:T(8,128)(2,1)S(1)} %pad_maximum_fusion.3), channel_id=1, source_target_pairs={{0,4},{4,0},{8,12},{12,8},{16,20},{20,16},{24,28},{28,24},{1,5},{5... | collective-permute-start | bytes 4718600 | tf_op jit(solution)/shard_map/ppermute | solution.py:40
  166.3 12.2 %collective-permute-start.14 = (bf16[1,1,4,32,3072]{4,3,2,1,0:T(8,128)(2,1)S(1)}, bf16[1,1,4,32,3072]{4,3,2,1,0:T(8,128)(2,1)}, u32[]{:S(2)}, u32[]{:S(2)}) collective-permute-start(bf16[1,1,4,32,3072]{4,3,2,1,0:T(8,128)(2,1)S(1)} %fusion.45), channel_id=1, source_target_pairs={{0,16},{4,12},{8,24},{12,4},{16,0},{20,28},{24,8},{28,20},{1,17},{... | collective-permute-start | bytes 2359304 | tf_op jit(solution)/shard_map/ppermute | solution.py:43
  168.4 8.6 %slice-start.3 = ((s8[9437184]{0:T(1024)(128)(4,1)}), s8[4194304]{0:T(1024)(128)(4,1)S(1)}, s32[]{:S(2)}) async-start(s8[9437184]{0:T(1024)(128)(4,1)} %bitcast.132), calls=%async_computation.6 | async-start | bytes 8388608
  168.4 8.6 %slice-start.4 = ((s8[9437184]{0:T(1024)(128)(4,1)}), s8[4194304]{0:T(1024)(128)(4,1)S(1)}, s32[]{:S(2)}) async-start(s8[9437184]{0:T(1024)(128)(4,1)} %bitcast.132), calls=%async_computation.7 | async-start | bytes 8388608
  179.8 27.3 %collective-permute-start.17 = (bf16[1,2,4,32,1536]{4,3,2,1,0:T(8,128)(2,1)S(1)}, bf16[1,2,4,32,1536]{4,3,2,1,0:T(8,128)(2,1)}, u32[]{:S(2)}, u32[]{:S(2)}) collective-permute-start(bf16[1,2,4,32,1536]{4,3,2,1,0:T(8,128)(2,1)S(1)} %get-tuple-element.15), channel_id=1, source_target_pairs={{0,8},{4,20},{8,0},{12,28},{16,24},{20,4},{24,16},{28,12},{1,9},{5... | collective-permute-start | bytes 2359304 | tf_op jit(solution)/shard_map/ppermute | solution.py:43
  181.3 19.1 %collective-permute-start.15 = (bf16[1,2,4,32,1536]{4,3,2,1,0:T(8,128)(2,1)S(1)}, bf16[1,2,4,32,1536]{4,3,2,1,0:T(8,128)(2,1)}, u32[]{:S(2)}, u32[]{:S(2)}) collective-permute-start(bf16[1,2,4,32,1536]{4,3,2,1,0:T(8,128)(2,1)S(1)} %get-tuple-element.16), channel_id=1, source_target_pairs={{0,8},{4,20},{8,0},{12,28},{16,24},{20,4},{24,16},{28,12},{1,9},{5... | collective-permute-start | bytes 2359304 | tf_op jit(solution)/shard_map/ppermute | solution.py:43
  202.8 18.3 %collective-permute-start.16 = (bf16[2,2,4,32,1536]{4,3,2,1,0:T(8,128)(2,1)}, bf16[2,2,4,32,1536]{4,3,2,1,0:T(8,128)(2,1)}, u32[]{:S(2)}, u32[]{:S(2)}) collective-permute-start(bf16[2,2,4,32,1536]{4,3,2,1,0:T(8,128)(2,1)} %pad_maximum_fusion.6), channel_id=1, source_target_pairs={{0,4},{4,0},{8,12},{12,8},{16,20},{20,16},{24,28},{28,24},{1,5},{5... | collective-permute-start | bytes 4718600 | tf_op jit(solution)/shard_map/ppermute | solution.py:40
  209.5 20.0 %collective-permute-start.18 = (bf16[2,2,4,32,1536]{4,3,2,1,0:T(8,128)(2,1)}, bf16[2,2,4,32,1536]{4,3,2,1,0:T(8,128)(2,1)}, u32[]{:S(2)}, u32[]{:S(2)}) collective-permute-start(bf16[2,2,4,32,1536]{4,3,2,1,0:T(8,128)(2,1)} %pad_maximum_fusion.7), channel_id=1, source_target_pairs={{0,4},{4,0},{8,12},{12,8},{16,20},{20,16},{24,28},{28,24},{1,5},{5... | collective-permute-start | bytes 4718600 | tf_op jit(solution)/shard_map/ppermute | solution.py:40
  (17 other events, 80.0 us)
Sparse Core Ops, SparseCore 0:
  21.7 39.4 all-gather.1
  187.7 21.9 reduce-scatter.1
where the time goes:
time: 245 us; the launch traced here: 241 us
  waiting for transfers between devices  99.3 us (41%)
  matrix products  65.4 us (27%)
  other arithmetic  30.7 us (13%)
  starting transfers between devices  19.6 us (8%)
  between operations  15.1 us (6%)
  local copies, waits for them, and re-layouts  10.8 us (4%)
    ppermute x12, waiting for transfers between devices, swap_chip(): lax.ppermute(v, 'row', [(i, i ^ 1 << orders[i & 1][step]) for i in range(...  64.1 us
    all_gather x1, waiting for transfers between devices, per_device(): every = lax.all_gather(mine, 'col', axis=steps, tiled=True)  30.7 us
    ppermute x12, starting transfers between devices, swap_chip(): lax.ppermute(v, 'row', [(i, i ^ 1 << orders[i & 1][step]) for i in range(...  17.7 us
    dot_general x4, matrix products, weight_grad(): out = jnp.dot(rows, piece, preferred_element_type=f32).astype(bf16)  16.9 us
    dot_general x4, matrix products, weight_grad(): lax.dot_general(piece, rows, (((0,), (0,)), ((), ())), preferred_element_...  13.4 us
    dot_general x4, matrix products, down(): out = jnp.dot(piece, block, preferred_element_type=f32)  12.8 us
    dot_general x4, matrix products, back(): lax.dot_general(flat(c), w_out[h], (((1,), (1,)), ((), ())), preferred_el...  12.1 us
    dot_general x4, matrix products, up(): jnp.dot(flat(x), w_in[:, h], preferred_element_type=f32)  10.2 us
  transfers between devices with their start and end apart: 21, of which 8 were waited for; matrix products, arithmetic and copies ran while one was open for 31% of the time, Pallas kernels for 0%

commit v1 on v0

v1 whole, which is shorter than its diff:
```python
import jax
import jax.numpy as jnp
from jax import lax
from jax.sharding import PartitionSpec as P

f32 = jnp.float32
bf16 = jnp.bfloat16


def gelu_parts(hidden):
    cdf = 0.5 * (1.0 + jax.scipy.special.erf(hidden * 0.7071067811865476))
    pdf = jnp.exp(-0.5 * hidden * hidden) * 0.3989422804014327
    return (hidden * cdf, cdf + hidden * pdf)


def terms(plain, turned, w, core, back):
    cut = w.shape[0 if back else 1] // 2
    if back:
        out = [
            lax.dot_general(v, w[h * cut : (h + 1) * cut], (((1,), (1,)), ((), ())), preferred_element_type=f32)
            for h, v in enumerate((plain, turned))
        ]
    else:
        out = [
            jnp.dot(v, w[:, h * cut : (h + 1) * cut], preferred_element_type=f32)
            for h, v in enumerate((plain, turned))
        ]
    out = [v.astype(bf16) for v in out]
    return jnp.where(core == 0, out[0], out[1]), jnp.where(core == 0, out[1], out[0])


def add_and_split(v, got):
    rows = v.shape[0]
    total = (v.astype(f32) + got.astype(f32)).astype(bf16)
    return total[: rows // 2], total[rows // 2 :]


def weight_grad(piece, rows, half, p, into, across):
    quarter = piece.shape[1]
    at = (half * 2 + p) * quarter
    if across:
        out = jnp.dot(rows, piece, preferred_element_type=f32).astype(bf16)
        return lax.dynamic_update_slice(into, out, (0, at))
    out = lax.dot_general(piece, rows, (((0,), (0,)), ((), ())), preferred_element_type=f32).astype(bf16)
    return lax.dynamic_update_slice(into, out, (at, 0))


def down(piece, w_out, half, p, add):
    quarter = piece.shape[1]
    block = lax.dynamic_slice_in_dim(w_out, (half * 2 + p) * quarter, quarter, 0)
    out = jnp.dot(piece, block, preferred_element_type=f32)
    return out if add is None else add + out


def make(n_row, n_col):
    row_bits = n_row.bit_length() - 1
    col_bits = n_col.bit_length() - 1
    first = tuple(range(1, row_bits))
    orders = (first, first[::-1])
    steps = len(first)

    def swap_core(v):
        return lax.ppermute(v, "row", [(i, i ^ 1) for i in range(n_row)])

    def swap_chip(v, step):
        return lax.ppermute(v, "row", [(i, i ^ (1 << orders[i & 1][step])) for i in range(n_row)])

    def swap_col(v, bit):
        return lax.ppermute(v, "col", [(i, i ^ (1 << bit)) for i in range(n_col)])

    def part(v, axis, index):
        return lax.slice_in_dim(v, index, index + 1, axis=axis)

    def flips(v, order, axis):
        me = lax.axis_index("row")
        for k, bit in enumerate(order):
            v = jnp.where((me >> bit) & 1 == 1, jnp.flip(v, axis + k), v)
        return v

    def relative(v):
        v = v.reshape((2,) * steps + (1, v.shape[0] >> steps, v.shape[1]))
        return flips(v, first, 0)

    def turn(v):
        return v.transpose(tuple(range(steps))[::-1] + tuple(range(steps, v.ndim)))

    def after(v, *tokens):
        return lax.optimization_barrier((v,) + tokens)[0]

    def flat(v):
        return v.reshape(-1, v.shape[-1])

    def per_device(latents, w_in, w_out, cotangent):
        tokens, width = latents.shape
        cut = w_in.shape[1] // 2
        core = lax.axis_index("row") & 1
        own_half = core.astype(jnp.int32)
        other_half = 1 - own_half

        taken = []

        def take(got, *also):
            got = after(got, *taken, *also)
            taken[:] = [got]
            return got

        def up(x):
            own, other = terms(flat(x), flat(turn(x)), w_in, own_half, False)
            return own, swap_core(other)

        def back(c):
            own, other = terms(flat(c), flat(turn(c)), w_out, own_half, True)
            return own, swap_core(other)

        def step(keep, got, k):
            keep, send = add_and_split(keep, got)
            return keep, swap_chip(send, k)

        def total(keep, got):
            return (keep.astype(f32) + got.astype(f32)).reshape((1,) * steps + (-1, tokens >> steps, cut))

        def double(v, got):
            return lax.concatenate([v, got], steps)

        def steps_on(flight, begin, end):
            for k in range(begin, end):
                flight = step(flight[0], take(flight[1]), k)
            return flight

        both = lax.concatenate([relative(latents), relative(cotangent)], steps + 2)
        both = double(both, take(swap_col(both, 0)))
        x_all, c_all = both[..., :width], both[..., width:]
        hid = up(x_all)
        grad = back(c_all)
        x_next = swap_col(x_all, 1) if col_bits > 1 else None
        hid = step(hid[0], take(hid[1]), 0)
        grad = step(grad[0], take(grad[1]), 0)
        hids, grads = [], []
        for bit in range(1, col_bits):
            hid = hid[0], take(hid[1])
            x = take(x_next)
            grad = grad[0], take(grad[1])
            hid = step(*hid, 1) if steps > 1 else hid
            hid_new = up(after(x, grad[1]))
            grad = step(*grad, 1) if steps > 1 else grad
            c_next = swap_col(after(c_all, x), bit)
            x_all = double(x_all, x)
            x_next = swap_col(x_all, bit + 1) if bit + 1 < col_bits else None
            hid_new = step(hid_new[0], take(hid_new[1]), 0)
            hid = steps_on(hid, 2, steps)
            hids.append(total(hid[0], take(hid[1])))
            grad = steps_on(grad, 2, steps)
            grads.append(total(grad[0], take(grad[1])))
            c = take(c_next)
            c_all = double(c_all, c)
            hid = hid_new[0], take(hid_new[1])
            grad = back(after(c, hid[1]))
            if bit + 1 < col_bits:
                grad = step(grad[0], take(grad[1]), 0)
        if col_bits > 1:
            hid = step(*hid, 1)
            grad = step(grad[0], take(grad[1]), 0)
        hid = steps_on(hid, 2, steps)

        hids.append(total(hid[0], take(hid[1])))
        hid = lax.concatenate(hids, steps)
        act = gelu_parts(hid)[0].astype(bf16)

        def doubled(flight, k):
            return lax.concatenate([flight[0], take(flight[1])], k)

        def chips(v, begin, end):
            flight = v, swap_chip(v, end - 1)
            for k in reversed(range(begin, end - 1)):
                v = doubled(flight, k + 1)
                flight = v, swap_chip(v, k)
            return flight

        quarter = cut // 2

        def quarters(v):
            return [v[..., p * quarter : (p + 1) * quarter] for p in range(2)]

        act = chips(act, 1, steps)
        grad = steps_on(grad, 1, steps)
        act = quarters(doubled(act, 1))
        acts = [(v, swap_chip(v, 0)) for v in act]
        grads.append(total(grad[0], take(grad[1])))
        grad = lax.concatenate(grads, steps)
        hid, grad = lax.optimization_barrier((hid, grad))
        grad = chips((grad * gelu_parts(hid)[1]).astype(bf16), 1, steps)

        x_turned, c_turned = turn(x_all), turn(c_all)

        def ordered(plain, turned, half):
            return jnp.where(half == 0, flat(plain), flat(turned))

        x_rows = [lax.optimization_barrier(ordered(x_all, x_turned, h).T) for h in (own_half, other_half)]
        c_rows = [lax.optimization_barrier(ordered(c_all, c_turned, h)) for h in (own_half, other_half)]

        acts[0] = doubled(acts[0], 0)
        acts[0] = acts[0], swap_core(acts[0])
        acts[1] = doubled(acts[1], 0)
        acts[1] = acts[1], swap_core(acts[1])
        acts[0] = acts[0][0], take(acts[0][1])
        grad = quarters(doubled(grad, 1))
        grads = [(v, swap_chip(v, 0)) for v in grad]
        acts[1] = acts[1][0], take(acts[1][1])

        sums = [None, None]
        for p in range(2):
            for i, half in enumerate((own_half, other_half)):
                sums[i] = down(flat(acts[p][i]), w_out, half, p, sums[i])
        sums = [v.reshape(x_all.shape) for v in sums]
        mixed = jnp.where(core == 0, sums[0], sums[1]) + turn(jnp.where(core == 0, sums[1], sums[0]))
        mixed = mixed.astype(bf16)

        def halve(mixed, bit):
            blocks = mixed.shape[steps]
            mixed = mixed.reshape(mixed.shape[:steps] + (blocks // 2, 2) + mixed.shape[steps + 1 :])
            return (
                lax.index_in_dim(mixed, 0, steps + 1, False),
                swap_col(lax.index_in_dim(mixed, 1, steps + 1, False), bit),
            )

        def merged(flight):
            return (flight[0].astype(f32) + take(flight[1]).astype(f32)).astype(bf16)

        mixed = halve(mixed, 0)
        grad_w_out = jnp.zeros_like(w_out)
        for i, half in enumerate((own_half, other_half)):
            grad_w_out = weight_grad(flat(acts[0][i]), c_rows[i], half, 0, grad_w_out, False)
        grads[0] = lax.concatenate([grads[0][0], take(grads[0][1], grad_w_out)], 0)
        grads[0] = grads[0], swap_core(grads[0])
        for bit in range(1, col_bits):
            mixed = halve(merged(mixed), bit)
        for i, half in enumerate((own_half, other_half)):
            grad_w_out = weight_grad(flat(acts[1][i]), c_rows[i], half, 1, grad_w_out, False)
        grads[1] = lax.concatenate([grads[1][0], take(grads[1][1], grad_w_out)], 0)
        grads[1] = grads[1], swap_core(grads[1])
        grads[0] = grads[0][0], take(grads[0][1])
        grad_w_in = jnp.zeros_like(w_in)
        for p, i in ((0, 0), (0, 1), (1, 0)):
            grad_w_in = weight_grad(flat(grads[p][i]), x_rows[i], (own_half, other_half)[i], p, grad_w_in, True)
        mixed = flips(merged(mixed), first, 0).reshape(tokens, width)
        grad_w_in = weight_grad(flat(take(grads[1][1])), x_rows[1], other_half, 1, grad_w_in, True)
        return (mixed, grad_w_in, grad_w_out)

    return per_device


def solution(mesh):
    placed = (P("col", "row"), P("row", "col"), P("col", "row"), P("col", "row"))
    return jax.shard_map(
        make(mesh.shape["row"], mesh.shape["col"]),
        mesh=mesh,
        in_specs=placed,
        out_specs=(P("col", "row"), P("row", "col"), P("col", "row")),
        check_vma=False,
    )
```

time: 245 us -> 207 us (0.84); the launches traced: 241 us -> 206 us
  matrix products: 65.4 us -> 49 us
  between operations: 15.1 us -> 1.42 us
  other arithmetic: 30.7 us -> 17.7 us
  starting transfers between devices: 19.6 us -> 28.3 us
    ppermute x0 -> x5, waiting for transfers between devices: none -> 37.8 us  [swap_col(): return lax.ppermute(v, 'col', [(i, i ^ 1 << bit) for i in range(n_col)])]
    all_gather x1 -> x0, waiting for transfers between devices: 30.7 us -> none  [per_device(): every = lax.all_gather(mine, 'col', axis=steps, tiled=True)]
    ppermute x0 -> x5, starting transfers between devices: none -> 10.4 us  [swap_col(): return lax.ppermute(v, 'col', [(i, i ^ 1 << bit) for i in range(n_col)])]
    concatenate x11 -> x10, other arithmetic: 12.1 us -> 3.55 us  [the longest x1 1.41 us: per_device(): grads[1] = lax.concatenate([grads[1][0], take(grads[1][1], grad_w_out)], 0)]
    dot_general x4, matrix products: 13.4 us -> 7.33 us  [weight_grad(): lax.dot_general(piece, rows, (((0,), (0,)), ((), ())), preferred_element_...]
    dot_general x4, matrix products: 16.9 us -> 11.7 us  [weight_grad(): out = jnp.dot(rows, piece, preferred_element_type=f32).astype(bf16)]
    ppermute x12 -> x14, waiting for transfers between devices: 64.1 us -> 59.4 us  [swap_chip(): lax.ppermute(v, 'row', [(i, i ^ 1 << orders[i & 1][step]) for i in range(...]
    unnamed x40 -> x47, local copies, waits for them, and re-layouts: 2.01 us -> 6.32 us
  transfers between devices with their start and end apart: 21 -> 27, of which waited for: 8 -> 15; matrix products, arithmetic and copies ran while one was open for 31% -> 20% of each run, Pallas kernels for 0% -> 0%
where the time goes in v1:
time: 207 us; the launch traced here: 206 us
  waiting for transfers between devices  100 us (48%)
  matrix products  49 us (24%)
  starting transfers between devices  28.3 us (14%)
  other arithmetic  17.7 us (9%)
  local copies, waits for them, and re-layouts  9.58 us (5%)
    ppermute x14, waiting for transfers between devices, swap_chip(): lax.ppermute(v, 'row', [(i, i ^ 1 << orders[i & 1][step]) for i in range(...  59.4 us
    ppermute x5, waiting for transfers between devices, swap_col(): return lax.ppermute(v, 'col', [(i, i ^ 1 << bit) for i in range(n_col)])  37.8 us
    ppermute x14, starting transfers between devices, swap_chip(): lax.ppermute(v, 'row', [(i, i ^ 1 << orders[i & 1][step]) for i in range(...  16.3 us
    dot_general x4, matrix products, weight_grad(): out = jnp.dot(rows, piece, preferred_element_type=f32).astype(bf16)  11.7 us
    dot_general x4, matrix products, terms(): lax.dot_general(v, w[h * cut:(h + 1) * cut], (((1,), (1,)), ((), ())), pr...  10.7 us
    ppermute x5, starting transfers between devices, swap_col(): return lax.ppermute(v, 'col', [(i, i ^ 1 << bit) for i in range(n_col)])  10.4 us
    dot_general x4, matrix products, terms(): jnp.dot(v, w[:, h * cut:(h + 1) * cut], preferred_element_type=f32)  10 us
    dot_general x4, matrix products, down(): out = jnp.dot(piece, block, preferred_element_type=f32)  9.3 us
  transfers between devices with their start and end apart: 27, of which 15 were waited for; matrix products, arithmetic and copies ran while one was open for 20% of the time, Pallas kernels for 0%

profile of v1, /device:TPU:0, one launch (start us, length us, event | category | flops | bytes accessed | tf_op | source)
XLA Modules:
  0.0 206.3 jit_solution(8929833393683980910)
XLA Ops:
  2.1 3.1 %collective-permute-start = (bf16[2,2,1,32,1536]{4,3,2,1,0:T(8,128)(2,1)S(1)}, bf16[2,2,1,32,1536]{4,3,2,1,0:T(8,128)(2,1)S(1)}, u32[]{:S(2)}, u32[]{:S(2)}) collective-permute-start(bf16[2,2,1,32,1536]{4,3,2,1,0:T(8,128)(2,1)S(1)} %pad_maximum_fusion.11), channel_id=1, source_target_pairs={{0,1},{1,0},{2,3},{3,2},{4,5},{5,4},{6,7},{7,6},{8,9},{9,8},{10,11... | collective-permute-start | bytes 1179656 | tf_op jit(solution)/shard_map/ppermute | solution.py:69
  5.2 9.1 %collective-permute-done = bf16[2,2,1,32,1536]{4,3,2,1,0:T(8,128)(2,1)S(1)} collective-permute-done((bf16[2,2,1,32,1536]{4,3,2,1,0:T(8,128)(2,1)S(1)}, bf16[2,2,1,32,1536]{4,3,2,1,0:T(8,128)(2,1)S(1)}, u32[]{:S(2)}, u32[]{:S(2)}) %collective-permute-start) | collective-permute-done | bytes 393248 | tf_op jit(solution)/shard_map/ppermute | solution.py:69
  14.6 4.0 %fusion.16 = bf16[256,3072]{1,0:T(8,128)(2,1)S(1)} fusion(bf16[256,768]{1,0:T(8,128)(2,1)S(1)} %bitcast.110, bf16[768,6144]{1,0:T(8,128)(2,1)} %param.5), kind=kOutput, calls=%fused_computation.16 | convolution fusion | flops 1208745984 | bytes 6684672 | tf_op jit(solution)/shard_map/dot_general | solution.py:25
  34.1 4.4 %collective-permute-done.2 = bf16[128,3072]{1,0:T(8,128)(2,1)S(1)} collective-permute-done((bf16[128,3072]{1,0:T(8,128)(2,1)S(1)}, bf16[128,3072]{1,0:T(8,128)(2,1)S(1)}, u32[]{:S(2)}, u32[]{:S(2)}) %collective-permute-start.2) | collective-permute-done | bytes 786464 | tf_op jit(solution)/shard_map/ppermute | solution.py:66
  38.5 13.3 %collective-permute-done.5 = bf16[2,2,2,32,768]{4,3,2,1,0:T(8,128)(2,1)S(1)} collective-permute-done((bf16[2,2,2,32,768]{4,3,2,1,0:T(8,128)(2,1)S(1)}, bf16[2,2,2,32,768]{4,3,2,1,0:T(8,128)(2,1)S(1)}, u32[]{:S(2)}, u32[]{:S(2)}) %collective-permute-start.5) | collective-permute-done | bytes 393248 | tf_op jit(solution)/shard_map/ppermute | solution.py:69
  53.3 3.2 %broadcast_select_fusion.1 = (bf16[256,3072]{1,0:T(8,128)(2,1)}, bf16[256,3072]{1,0:T(8,128)(2,1)}) fusion(bf16[256,3072]{1,0:T(8,128)(2,1)S(1)} %fusion.19, pred[]{:T(512)S(6)} %eq.10, bf16[256,768]{1,0:T(8,128)(2,1)S(1)} %bitcast.132, bf16[768,6144]{1,0:T(8,128)(2,1)S(1)} %copy-done.16), kind=kOutput, calls=%fused_computation.77 | convolution fusion | flops 1209532416 | bytes 9830401 | tf_op jit(solution)/shard_map/dot_general | solution.py:25
  64.2 10.5 %collective-permute-done.4 = bf16[64,3072]{1,0:T(8,128)(2,1)S(1)} collective-permute-done((bf16[64,3072]{1,0:T(8,128)(2,1)S(1)}, bf16[64,3072]{1,0:T(8,128)(2,1)S(1)}, u32[]{:S(2)}, u32[]{:S(2)}) %collective-permute-start.4) | collective-permute-done | bytes 393248 | tf_op jit(solution)/shard_map/ppermute | solution.py:66
  77.9 4.0 %fusion.37 = bf16[256,3072]{1,0:T(8,128)(2,1)S(1)} fusion(bf16[256,768]{1,0:T(8,128)(2,1)S(1)} %bitcast.113, bf16[6144,768]{1,0:T(8,128)(2,1)} %param.6), kind=kOutput, calls=%fused_computation.23 | convolution fusion | flops 1208745984 | bytes 6684672 | tf_op jit(solution)/shard_map/dot_general | solution.py:20
  81.9 3.8 %broadcast_select_fusion = (bf16[256,3072]{1,0:T(8,128)(2,1)S(1)}, bf16[256,3072]{1,0:T(8,128)(2,1)S(1)}) fusion(bf16[256,3072]{1,0:T(8,128)(2,1)S(1)} %fusion.37, pred[]{:T(512)S(6)} %eq.10, bf16[256,768]{1,0:T(8,128)(2,1)S(1)} %bitcast.133, bf16[6144,768]{1,0:T(8,128)(2,1)} %param.6), kind=kOutput, calls=%fused_computation.76 | convolution fusion | flops 1209532416 | bytes 9830401 | tf_op jit(solution)/shard_map/dot_general | solution.py:20
  89.3 5.0 %collective-permute-done.11 = bf16[64,3072]{1,0:T(8,128)(2,1)S(1)} collective-permute-done((bf16[64,3072]{1,0:T(8,128)(2,1)S(1)}, bf16[64,3072]{1,0:T(8,128)(2,1)S(1)}, u32[]{:S(2)}, u32[]{:S(2)}) %collective-permute-start.11) | collective-permute-done | bytes 393248 | tf_op jit(solution)/shard_map/ppermute | solution.py:66
  97.7 17.7 %collective-permute-done.14 = bf16[128,3072]{1,0:T(8,128)(2,1)S(1)} collective-permute-done((bf16[128,3072]{1,0:T(8,128)(2,1)S(1)}, bf16[128,3072]{1,0:T(8,128)(2,1)S(1)}, u32[]{:S(2)}, u32[]{:S(2)}) %collective-permute-start.14) | collective-permute-done | bytes 786464 | tf_op jit(solution)/shard_map/ppermute | solution.py:66
  119.4 8.4 %collective-permute-done.16 = bf16[64,3072]{1,0:T(8,128)(2,1)S(1)} collective-permute-done((bf16[64,3072]{1,0:T(8,128)(2,1)S(1)}, bf16[64,3072]{1,0:T(8,128)(2,1)S(1)}, u32[]{:S(2)}, u32[]{:S(2)}) %collective-permute-start.16) | collective-permute-done | bytes 393248 | tf_op jit(solution)/shard_map/ppermute | solution.py:66
  128.0 9.8 %collective-permute-done.15 = bf16[1,2,4,32,1536]{4,3,2,1,0:T(8,128)(2,1)S(1)} collective-permute-done((bf16[1,2,4,32,1536]{4,3,2,1,0:T(8,128)(2,1)S(1)}, bf16[1,2,4,32,1536]{4,3,2,1,0:T(8,128)(2,1)S(1)}, u32[]{:S(2)}, u32[]{:S(2)}) %collective-permute-start.15) | collective-permute-done | bytes 786464 | tf_op jit(solution)/shard_map/ppermute | solution.py:66
  143.1 3.7 %fusion.52 = f32[512,768]{1,0:T(8,128)S(1)} fusion(bf16[512,1536]{1,0:T(8,128)(2,1)S(1)} %bitcast.105, bf16[6144,768]{1,0:T(8,128)(2,1)} %param.6, s32[]{:T(128)S(6)} %select_n.155), kind=kOutput, calls=%fused_computation.49 | convolution fusion | flops 1207959552 | bytes 5505028 | tf_op jit(solution)/shard_map/dot_general | solution.py:51
  148.3 3.1 %collective-permute-done.20 = bf16[1,1,4,32,3072]{4,3,2,1,0:T(8,128)(2,1)S(1)} collective-permute-done((bf16[1,1,4,32,3072]{4,3,2,1,0:T(8,128)(2,1)S(1)}, bf16[1,1,4,32,3072]{4,3,2,1,0:T(8,128)(2,1)S(1)}, u32[]{:S(2)}, u32[]{:S(2)}) %collective-permute-start.20) | collective-permute-done | bytes 786464 | tf_op jit(solution)/shard_map/ppermute | solution.py:66
  157.9 4.1 %collective-permute-start.21 = (bf16[2,2,2,32,768]{4,3,1,0,2:T(8,128)(2,1)S(1)}, bf16[2,2,2,32,768]{4,3,1,0,2:T(8,128)(2,1)S(1)}, u32[]{:S(2)}, u32[]{:S(2)}) collective-permute-start(bf16[2,2,2,32,768]{4,3,1,0,2:T(8,128)(2,1)S(1)} %bitcast.129), channel_id=1, source_target_pairs={{0,1},{1,0},{2,3},{3,2},{4,5},{5,4},{6,7},{7,6},{8,9},{9,8},{10,11... | collective-permute-start | bytes 1179656 | tf_op jit(solution)/shard_map/ppermute | solution.py:69
  165.5 5.0 %collective-permute-done.21 = bf16[2,2,2,32,768]{4,3,1,0,2:T(8,128)(2,1)S(1)} collective-permute-done((bf16[2,2,2,32,768]{4,3,1,0,2:T(8,128)(2,1)S(1)}, bf16[2,2,2,32,768]{4,3,1,0,2:T(8,128)(2,1)S(1)}, u32[]{:S(2)}, u32[]{:S(2)}) %collective-permute-start.21) | collective-permute-done | bytes 393248 | tf_op jit(solution)/shard_map/ppermute | solution.py:69
  171.9 2.8 %fusion.44 = bf16[6144,768]{1,0:T(8,128)(2,1)S(1)} fusion(bf16[6144,768]{1,0:T(8,128)(2,1)S(1)} %fusion.45, s32[]{:T(128)S(6)} %select_n.157, bf16[512,1536]{1,0:T(8,128)(2,1)} %bitcast.21, bf16[512,768]{1,0:T(8,128)(2,1)S(1)} %bitcast.118), kind=kOutput, calls=%fused_computation.33 | convolution fusion | flops 1209139200 | bytes 4718596 | tf_op jit(solution)/shard_map/dot_general | solution.py:44
  181.2 3.1 %fusion.43 = bf16[768,6144]{1,0:T(8,128)(2,1)S(1)} fusion(bf16[768,6144]{1,0:T(8,128)(2,1)S(1)} %broadcast_in_dim.7, s32[]{:T(128)S(6)} %select_n.154, bf16[768,512]{0,1:T(8,128)(2,1)} %bitcast.123, bf16[512,1536]{1,0:T(8,128)(2,1)} %bitcast.39), kind=kOutput, calls=%fused_computation.31 | convolution fusion | flops 1209139200 | bytes 4718596 | tf_op jit(solution)/shard_map/dot_general | solution.py:42
  184.4 7.8 %collective-permute-done.23 = bf16[2,2,1,32,768]{4,3,2,1,0:T(8,128)(2,1)} collective-permute-done((bf16[2,2,1,32,768]{4,3,2,1,0:T(8,128)(2,1)}, bf16[2,2,1,32,768]{4,3,2,1,0:T(8,128)(2,1)}, u32[]{:S(2)}, u32[]{:S(2)}) %collective-permute-start.23) | collective-permute-done | bytes 196640 | tf_op jit(solution)/shard_map/ppermute | solution.py:69
  193.9 2.9 %fusion.42 = bf16[768,6144]{1,0:T(8,128)(2,1)S(1)} fusion(bf16[768,6144]{1,0:T(8,128)(2,1)S(1)} %fusion.43, s32[]{:T(128)S(6)} %select_n.156, bf16[768,512]{0,1:T(8,128)(2,1)S(1)} %bitcast.121, bf16[512,1536]{1,0:T(8,128)(2,1)} %bitcast.42), kind=kOutput, calls=%fused_computation.29 | convolution fusion | flops 1209139200 | bytes 4718596 | tf_op jit(solution)/shard_map/dot_general | solution.py:42
  196.9 2.8 %fusion.41 = bf16[768,6144]{1,0:T(8,128)(2,1)S(1)} fusion(bf16[768,6144]{1,0:T(8,128)(2,1)S(1)} %fusion.42, s32[]{:T(128)S(6)} %select_n.155, bf16[768,512]{0,1:T(8,128)(2,1)S(1)} %bitcast.124, bf16[512,1536]{1,0:T(8,128)(2,1)} %bitcast.43), kind=kOutput, calls=%fused_computation.27 | convolution fusion | flops 1209139200 | bytes 4718596 | tf_op jit(solution)/shard_map/dot_general | solution.py:42
  199.7 2.8 %fusion.40 = bf16[768,6144]{1,0:T(8,128)(2,1)S(1)} fusion(bf16[768,6144]{1,0:T(8,128)(2,1)S(1)} %fusion.41, s32[]{:T(128)S(6)} %select_n.157, bf16[768,512]{0,1:T(8,128)(2,1)S(1)} %bitcast.122, bf16[512,1536]{1,0:T(8,128)(2,1)} %bitcast.44), kind=kOutput, calls=%fused_computation.25 | convolution fusion | flops 1209139200 | bytes 4718596 | tf_op jit(solution)/shard_map/dot_general | solution.py:42
  202.5 3.7 %copy-done = bf16[768,6144]{1,0:T(8,128)(2,1)} copy-done((bf16[768,6144]{1,0:T(8,128)(2,1)}, bf16[768,6144]{1,0:T(8,128)(2,1)S(1)}, u32[]{:S(2)}) %copy-start) | copy-done | bytes 9437208
  (151 shorter events, 66.7 us)
Async XLA Ops:
  2.1 12.2 %collective-permute-start = (bf16[2,2,1,32,1536]{4,3,2,1,0:T(8,128)(2,1)S(1)}, bf16[2,2,1,32,1536]{4,3,2,1,0:T(8,128)(2,1)S(1)}, u32[]{:S(2)}, u32[]{:S(2)}) collective-permute-start(bf16[2,2,1,32,1536]{4,3,2,1,0:T(8,128)(2,1)S(1)} %pad_maximum_fusion.11), channel_id=1, source_target_pairs={{0,1},{1,0},{2,3},{3,2},{4,5},{5,4},{6,7},{7,6},{8,9},{9,8},{10,11... | collective-permute-start | bytes 1179656 | tf_op jit(solution)/shard_map/ppermute | solution.py:69
  21.2 4.3 %collective-permute-start.1 = (bf16[256,3072]{1,0:T(8,128)(2,1)S(1)}, bf16[256,3072]{1,0:T(8,128)(2,1)S(1)}, u32[]{:S(2)}, u32[]{:S(2)}) collective-permute-start(bf16[256,3072]{1,0:T(8,128)(2,1)S(1)} %get-tuple-element.83), channel_id=1, source_target_pairs={{0,4},{4,0},{8,12},{12,8},{16,20},{20,16},{24,28},{28,24},{1,5},{5... | collective-permute-start | bytes 4718600 | tf_op jit(solution)/shard_map/ppermute | solution.py:63
  26.4 12.1 %collective-permute-start.2 = (bf16[128,3072]{1,0:T(8,128)(2,1)S(1)}, bf16[128,3072]{1,0:T(8,128)(2,1)S(1)}, u32[]{:S(2)}, u32[]{:S(2)}) collective-permute-start(bf16[128,3072]{1,0:T(8,128)(2,1)S(1)} %slice.126), channel_id=1, source_target_pairs={{0,8},{4,20},{8,0},{12,28},{16,24},{20,4},{24,16},{28,12},{1,9},{5... | collective-permute-start | bytes 2359304 | tf_op jit(solution)/shard_map/ppermute | solution.py:66
  29.8 22.0 %collective-permute-start.6 = (bf16[128,3072]{1,0:T(8,128)(2,1)S(1)}, bf16[128,3072]{1,0:T(8,128)(2,1)}, u32[]{:S(2)}, u32[]{:S(2)}) collective-permute-start(bf16[128,3072]{1,0:T(8,128)(2,1)S(1)} %slice.130), channel_id=1, source_target_pairs={{0,8},{4,20},{8,0},{12,28},{16,24},{20,4},{24,16},{28,12},{1,9},{5... | collective-permute-start | bytes 2359304 | tf_op jit(solution)/shard_map/ppermute | solution.py:66
  31.5 20.2 %collective-permute-start.5 = (bf16[2,2,2,32,768]{4,3,2,1,0:T(8,128)(2,1)S(1)}, bf16[2,2,2,32,768]{4,3,2,1,0:T(8,128)(2,1)S(1)}, u32[]{:S(2)}, u32[]{:S(2)}) collective-permute-start(bf16[2,2,2,32,768]{4,3,2,1,0:T(8,128)(2,1)S(1)} %get-tuple-element.82), channel_id=1, source_target_pairs={{0,2},{1,3},{2,0},{3,1},{4,6},{5,7},{6,4},{7,5},{8,10},{9,11},{10,... | collective-permute-start | bytes 1179656 | tf_op jit(solution)/shard_map/ppermute | solution.py:69
  56.5 20.9 %collective-permute-start.9 = (bf16[2,2,2,32,768]{4,3,2,1,0:T(8,128)(2,1)S(1)}, bf16[2,2,2,32,768]{4,3,2,1,0:T(8,128)(2,1)S(1)}, u32[]{:S(2)}, u32[]{:S(2)}) collective-permute-start(bf16[2,2,2,32,768]{4,3,2,1,0:T(8,128)(2,1)S(1)} %get-tuple-element.42), channel_id=1, source_target_pairs={{0,2},{1,3},{2,0},{3,1},{4,6},{5,7},{6,4},{7,5},{8,10},{9,11},{10,... | collective-permute-start | bytes 1179656 | tf_op jit(solution)/shard_map/ppermute | solution.py:69
  58.0 16.8 %collective-permute-start.10 = (bf16[64,3072]{1,0:T(8,128)(2,1)S(1)}, bf16[64,3072]{1,0:T(8,128)(2,1)S(1)}, u32[]{:S(2)}, u32[]{:S(2)}) collective-permute-start(bf16[64,3072]{1,0:T(8,128)(2,1)S(1)} %slice.134), channel_id=1, source_target_pairs={{0,16},{4,12},{8,24},{12,4},{16,0},{20,28},{24,8},{28,20},{1,17},{... | collective-permute-start | bytes 1179656 | tf_op jit(solution)/shard_map/ppermute | solution.py:66
  58.7 16.0 %collective-permute-start.4 = (bf16[64,3072]{1,0:T(8,128)(2,1)S(1)}, bf16[64,3072]{1,0:T(8,128)(2,1)S(1)}, u32[]{:S(2)}, u32[]{:S(2)}) collective-permute-start(bf16[64,3072]{1,0:T(8,128)(2,1)S(1)} %slice.129), channel_id=1, source_target_pairs={{0,16},{4,12},{8,24},{12,4},{16,0},{20,28},{24,8},{28,20},{1,17},{... | collective-permute-start | bytes 1179656 | tf_op jit(solution)/shard_map/ppermute | solution.py:66
  62.6 15.3 %collective-permute-start.8 = (bf16[128,3072]{1,0:T(8,128)(2,1)S(1)}, bf16[128,3072]{1,0:T(8,128)(2,1)S(1)}, u32[]{:S(2)}, u32[]{:S(2)}) collective-permute-start(bf16[128,3072]{1,0:T(8,128)(2,1)S(1)} %slice.132), channel_id=1, source_target_pairs={{0,8},{4,20},{8,0},{12,28},{16,24},{20,4},{24,16},{28,12},{1,9},{5... | collective-permute-start | bytes 2359304 | tf_op jit(solution)/shard_map/ppermute | solution.py:66
  86.4 7.8 %collective-permute-start.11 = (bf16[64,3072]{1,0:T(8,128)(2,1)S(1)}, bf16[64,3072]{1,0:T(8,128)(2,1)S(1)}, u32[]{:S(2)}, u32[]{:S(2)}) collective-permute-start(bf16[64,3072]{1,0:T(8,128)(2,1)S(1)} %slice.136), channel_id=1, source_target_pairs={{0,16},{4,12},{8,24},{12,4},{16,0},{20,28},{24,8},{28,20},{1,17},{... | collective-permute-start | bytes 1179656 | tf_op jit(solution)/shard_map/ppermute | solution.py:66
  95.1 20.3 %collective-permute-start.14 = (bf16[128,3072]{1,0:T(8,128)(2,1)S(1)}, bf16[128,3072]{1,0:T(8,128)(2,1)S(1)}, u32[]{:S(2)}, u32[]{:S(2)}) collective-permute-start(bf16[128,3072]{1,0:T(8,128)(2,1)S(1)} %slice.137), channel_id=1, source_target_pairs={{0,8},{4,20},{8,0},{12,28},{16,24},{20,4},{24,16},{28,12},{1,9},{5... | collective-permute-start | bytes 2359304 | tf_op jit(solution)/shard_map/ppermute | solution.py:66
  97.1 20.0 %collective-permute-start.13 = (bf16[1,1,4,32,3072]{4,3,2,1,0:T(8,128)(2,1)S(1)}, bf16[1,1,4,32,3072]{4,3,2,1,0:T(8,128)(2,1)S(1)}, u32[]{:S(2)}, u32[]{:S(2)}) collective-permute-start(bf16[1,1,4,32,3072]{4,3,2,1,0:T(8,128)(2,1)S(1)} %get-tuple-element.70), channel_id=1, source_target_pairs={{0,16},{4,12},{8,24},{12,4},{16,0},{20,28},{24,8},{28,20},{1,17},{... | collective-permute-start | bytes 2359304 | tf_op jit(solution)/shard_map/ppermute | solution.py:66
  115.7 12.1 %collective-permute-start.16 = (bf16[64,3072]{1,0:T(8,128)(2,1)S(1)}, bf16[64,3072]{1,0:T(8,128)(2,1)S(1)}, u32[]{:S(2)}, u32[]{:S(2)}) collective-permute-start(bf16[64,3072]{1,0:T(8,128)(2,1)S(1)} %slice.141), channel_id=1, source_target_pairs={{0,16},{4,12},{8,24},{12,4},{16,0},{20,28},{24,8},{28,20},{1,17},{... | collective-permute-start | bytes 1179656 | tf_op jit(solution)/shard_map/ppermute | solution.py:66
  117.3 20.6 %collective-permute-start.17 = (bf16[1,2,4,32,1536]{4,3,2,1,0:T(8,128)(2,1)S(1)}, bf16[1,2,4,32,1536]{4,3,2,1,0:T(8,128)(2,1)S(1)}, u32[]{:S(2)}, u32[]{:S(2)}) collective-permute-start(bf16[1,2,4,32,1536]{4,3,2,1,0:T(8,128)(2,1)S(1)} %get-tuple-element.72), channel_id=1, source_target_pairs={{0,8},{4,20},{8,0},{12,28},{16,24},{20,4},{24,16},{28,12},{1,9},{5... | collective-permute-start | bytes 2359304 | tf_op jit(solution)/shard_map/ppermute | solution.py:66
  119.1 18.7 %collective-permute-start.15 = (bf16[1,2,4,32,1536]{4,3,2,1,0:T(8,128)(2,1)S(1)}, bf16[1,2,4,32,1536]{4,3,2,1,0:T(8,128)(2,1)S(1)}, u32[]{:S(2)}, u32[]{:S(2)}) collective-permute-start(bf16[1,2,4,32,1536]{4,3,2,1,0:T(8,128)(2,1)S(1)} %get-tuple-element.71), channel_id=1, source_target_pairs={{0,8},{4,20},{8,0},{12,28},{16,24},{20,4},{24,16},{28,12},{1,9},{5... | collective-permute-start | bytes 2359304 | tf_op jit(solution)/shard_map/ppermute | solution.py:66
  138.1 13.5 %collective-permute-start.19 = (bf16[2,2,4,32,1536]{4,3,2,1,0:T(8,128)(2,1)S(1)}, bf16[2,2,4,32,1536]{4,3,2,1,0:T(8,128)(2,1)}, u32[]{:S(2)}, u32[]{:S(2)}) collective-permute-start(bf16[2,2,4,32,1536]{4,3,2,1,0:T(8,128)(2,1)S(1)} %pad_maximum_fusion.2), channel_id=1, source_target_pairs={{0,4},{4,0},{8,12},{12,8},{16,20},{20,16},{24,28},{28,24},{1,5},{5... | collective-permute-start | bytes 4718600 | tf_op jit(solution)/shard_map/ppermute | solution.py:63
  138.3 9.9 %collective-permute-start.18 = (bf16[2,2,4,32,1536]{4,3,2,1,0:T(8,128)(2,1)S(1)}, bf16[2,2,4,32,1536]{4,3,2,1,0:T(8,128)(2,1)S(1)}, u32[]{:S(2)}, u32[]{:S(2)}) collective-permute-start(bf16[2,2,4,32,1536]{4,3,2,1,0:T(8,128)(2,1)S(1)} %pad_maximum_fusion.1), channel_id=1, source_target_pairs={{0,4},{4,0},{8,12},{12,8},{16,20},{20,16},{24,28},{28,24},{1,5},{5... | collective-permute-start | bytes 4718600 | tf_op jit(solution)/shard_map/ppermute | solution.py:63
  139.3 12.1 %collective-permute-start.20 = (bf16[1,1,4,32,3072]{4,3,2,1,0:T(8,128)(2,1)S(1)}, bf16[1,1,4,32,3072]{4,3,2,1,0:T(8,128)(2,1)S(1)}, u32[]{:S(2)}, u32[]{:S(2)}) collective-permute-start(bf16[1,1,4,32,3072]{4,3,2,1,0:T(8,128)(2,1)S(1)} %fusion.61), channel_id=1, source_target_pairs={{0,16},{4,12},{8,24},{12,4},{16,0},{20,28},{24,8},{28,20},{1,17},{... | collective-permute-start | bytes 2359304 | tf_op jit(solution)/shard_map/ppermute | solution.py:66
  151.6 12.6 %collective-permute-start.22 = (bf16[1,2,4,32,1536]{4,3,2,1,0:T(8,128)(2,1)S(1)}, bf16[1,2,4,32,1536]{4,3,2,1,0:T(8,128)(2,1)S(1)}, u32[]{:S(2)}, u32[]{:S(2)}) collective-permute-start(bf16[1,2,4,32,1536]{4,3,2,1,0:T(8,128)(2,1)S(1)} %get-tuple-element.68), channel_id=1, source_target_pairs={{0,8},{4,20},{8,0},{12,28},{16,24},{20,4},{24,16},{28,12},{1,9},{5... | collective-permute-start | bytes 2359304 | tf_op jit(solution)/shard_map/ppermute | solution.py:66
  157.9 12.5 %collective-permute-start.21 = (bf16[2,2,2,32,768]{4,3,1,0,2:T(8,128)(2,1)S(1)}, bf16[2,2,2,32,768]{4,3,1,0,2:T(8,128)(2,1)S(1)}, u32[]{:S(2)}, u32[]{:S(2)}) collective-permute-start(bf16[2,2,2,32,768]{4,3,1,0,2:T(8,128)(2,1)S(1)} %bitcast.129), channel_id=1, source_target_pairs={{0,1},{1,0},{2,3},{3,2},{4,5},{5,4},{6,7},{7,6},{8,9},{9,8},{10,11... | collective-permute-start | bytes 1179656 | tf_op jit(solution)/shard_map/ppermute | solution.py:69
  162.0 12.8 %collective-permute-start.25 = (bf16[1,2,4,32,1536]{4,3,2,1,0:T(8,128)(2,1)S(1)}, bf16[1,2,4,32,1536]{4,3,2,1,0:T(8,128)(2,1)S(1)}, u32[]{:S(2)}, u32[]{:S(2)}) collective-permute-start(bf16[1,2,4,32,1536]{4,3,2,1,0:T(8,128)(2,1)S(1)} %get-tuple-element.67), channel_id=1, source_target_pairs={{0,8},{4,20},{8,0},{12,28},{16,24},{20,4},{24,16},{28,12},{1,9},{5... | collective-permute-start | bytes 2359304 | tf_op jit(solution)/shard_map/ppermute | solution.py:66
  170.5 13.9 %collective-permute-start.24 = (bf16[2,2,4,32,1536]{4,3,2,1,0:T(8,128)(2,1)}, bf16[2,2,4,32,1536]{4,3,2,1,0:T(8,128)(2,1)}, u32[]{:S(2)}, u32[]{:S(2)}) collective-permute-start(bf16[2,2,4,32,1536]{4,3,2,1,0:T(8,128)(2,1)} %pad_maximum_fusion.4), channel_id=1, source_target_pairs={{0,4},{4,0},{8,12},{12,8},{16,20},{20,16},{24,28},{28,24},{1,5},{5... | collective-permute-start | bytes 4718600 | tf_op jit(solution)/shard_map/ppermute | solution.py:63
  176.2 17.8 %collective-permute-start.26 = (bf16[2,2,4,32,1536]{4,3,2,1,0:T(8,128)(2,1)}, bf16[2,2,4,32,1536]{4,3,2,1,0:T(8,128)(2,1)}, u32[]{:S(2)}, u32[]{:S(2)}) collective-permute-start(bf16[2,2,4,32,1536]{4,3,2,1,0:T(8,128)(2,1)} %pad_maximum_fusion.5), channel_id=1, source_target_pairs={{0,4},{4,0},{8,12},{12,8},{16,20},{20,16},{24,28},{28,24},{1,5},{5... | collective-permute-start | bytes 4718600 | tf_op jit(solution)/shard_map/ppermute | solution.py:63
  179.5 12.7 %collective-permute-start.23 = (bf16[2,2,1,32,768]{4,3,2,1,0:T(8,128)(2,1)}, bf16[2,2,1,32,768]{4,3,2,1,0:T(8,128)(2,1)}, u32[]{:S(2)}, u32[]{:S(2)}) collective-permute-start(bf16[2,2,1,32,768]{4,3,2,1,0:T(8,128)(2,1)} %slice_bitcast_fusion), channel_id=1, source_target_pairs={{0,2},{1,3},{2,0},{3,1},{4,6},{5,7},{6,4},{7,5},{8,10},{9,11},{10,... | collective-permute-start | bytes 589832 | tf_op jit(solution)/shard_map/ppermute | solution.py:69
  (26 other events, 155.3 us)

commit v2 on v1

v2 whole, which is shorter than its diff:
```python
import jax
import jax.numpy as jnp
from jax import lax
from jax.sharding import PartitionSpec as P

f32 = jnp.float32
bf16 = jnp.bfloat16


def gelu_parts(hidden):
    cdf = 0.5 * (1.0 + jax.scipy.special.erf(hidden * 0.7071067811865476))
    pdf = jnp.exp(-0.5 * hidden * hidden) * 0.3989422804014327
    return (hidden * cdf, cdf + hidden * pdf)


def add_and_split(v, got):
    rows = v.shape[0]
    total = (v.astype(f32) + got.astype(f32)).astype(bf16)
    return total[: rows // 2], total[rows // 2 :]


def weight_grad(piece, rows, half, p, into, across):
    quarter = piece.shape[1]
    at = (half * 2 + p) * quarter
    if across:
        out = jnp.dot(rows, piece, preferred_element_type=f32).astype(bf16)
        return lax.dynamic_update_slice(into, out, (0, at))
    out = lax.dot_general(piece, rows, (((0,), (0,)), ((), ())), preferred_element_type=f32).astype(bf16)
    return lax.dynamic_update_slice(into, out, (at, 0))


def make(n_row, n_col):
    row_bits = n_row.bit_length() - 1
    col_bits = n_col.bit_length() - 1
    first = tuple(range(1, row_bits))
    orders = (first, first[::-1])
    steps = len(first)

    def swap_core(v):
        return lax.ppermute(v, "row", [(i, i ^ 1) for i in range(n_row)])

    def swap_chip(v, step):
        return lax.ppermute(v, "row", [(i, i ^ (1 << orders[i & 1][step])) for i in range(n_row)])

    def part(v, axis, index):
        return lax.slice_in_dim(v, index, index + 1, axis=axis)

    def flips(v, order, axis):
        me = lax.axis_index("row")
        for k, bit in enumerate(order):
            v = jnp.where((me >> bit) & 1 == 1, jnp.flip(v, axis + k), v)
        return v

    def relative(v):
        v = v.reshape((2,) * steps + (1, v.shape[0] >> steps, v.shape[1]))
        return flips(v, first, 0)

    def turn(v):
        return v.transpose(tuple(range(steps))[::-1] + tuple(range(steps, v.ndim)))

    def after(v, *tokens):
        return lax.optimization_barrier((v,) + tokens)[0]

    def flat(v):
        return v.reshape(-1, v.shape[-1])

    def per_device(latents, w_in, w_out, cotangent):
        tokens, width = latents.shape
        cut = w_in.shape[1] // 2
        core = lax.axis_index("row") & 1
        own_half = core.astype(jnp.int32)
        other_half = 1 - own_half

        taken = []

        def take(got, *also):
            got = after(got, *taken, *also)
            taken[:] = [got]
            return got

        def halves(w, axis):
            return lax.optimization_barrier(
                tuple(lax.dynamic_slice_in_dim(w, h * cut, cut, axis) for h in (own_half, other_half))
            )

        def ordered(v):
            plain, turned = flat(v), flat(turn(v))
            return jnp.where(core == 0, plain, turned), jnp.where(core == 0, turned, plain)

        w_in_own, w_in_other = halves(w_in, 1)
        w_out_own, w_out_other = halves(w_out, 0)

        def up(x):
            own, other = ordered(x)
            got = swap_core(jnp.dot(other, w_in_other, preferred_element_type=f32).astype(bf16))
            return jnp.dot(own, w_in_own, preferred_element_type=f32).astype(bf16), got

        def back(c):
            own, other = ordered(c)
            dims = (((1,), (1,)), ((), ()))
            got = swap_core(lax.dot_general(other, w_out_other, dims, preferred_element_type=f32).astype(bf16))
            return lax.dot_general(own, w_out_own, dims, preferred_element_type=f32).astype(bf16), got

        def step(keep, got, k):
            keep, send = add_and_split(keep, got)
            return keep, swap_chip(send, k)

        def total(keep, got):
            return (keep.astype(f32) + got.astype(f32)).reshape((1,) * steps + (-1, tokens >> steps, cut))

        def steps_on(flight, begin, end):
            for k in range(begin, end):
                flight = step(flight[0], take(flight[1]), k)
            return flight

        def reach(v, distance):
            return lax.ppermute(v, "col", [(i, i ^ distance) for i in range(n_col)])

        x_own, c_own = relative(latents), relative(cotangent)
        near = reach(lax.concatenate([x_own, c_own], steps + 2), 1)
        x_far = [reach(x_own, d) for d in range(2, n_col)]
        x_far, near = lax.optimization_barrier((x_far, near))
        x_near = lax.concatenate([x_own, near[..., :width]], steps)
        c_near = lax.concatenate([c_own, near[..., width:]], steps)
        x_far = lax.concatenate(x_far, steps)
        x_all = lax.concatenate([x_near, x_far], steps)
        hid_near, hid_far, grad_near = up(x_near), up(x_far), back(c_near)
        x_rows = [lax.optimization_barrier(v.T) for v in ordered(x_all)]

        hid_near = step(hid_near[0], take(hid_near[1]), 0)
        hid_far = step(hid_far[0], take(hid_far[1]), 0)
        grad_near = grad_near[0], take(grad_near[1])
        c_far = [reach(after(c_own, x_far), d) for d in range(2, n_col)]
        hid_near = step(hid_near[0], take(hid_near[1], *x_rows), 1)
        grad_near = step(*grad_near, 0)
        hid_far = step(hid_far[0], take(hid_far[1]), 1)
        hid_near = steps_on(hid_near, 2, steps)
        hids = [total(hid_near[0], take(hid_near[1]))]
        c_far = lax.concatenate([take(v) for v in c_far], steps)
        grad_far = back(c_far)
        c_all = lax.concatenate([c_near, c_far], steps)
        c_rows = [lax.optimization_barrier(v) for v in ordered(c_all)]
        grad_near = step(grad_near[0], take(grad_near[1]), 1)
        hid_far = steps_on(hid_far, 2, steps)
        hids.append(total(hid_far[0], take(hid_far[1])))
        hid = lax.concatenate(hids, steps)
        act = gelu_parts(hid)[0].astype(bf16)

        def doubled(flight, k):
            return lax.concatenate([flight[0], take(flight[1])], k)

        def chips(v, begin, end):
            flight = v, swap_chip(v, end - 1)
            for k in reversed(range(begin, end - 1)):
                v = doubled(flight, k + 1)
                flight = v, swap_chip(v, k)
            return flight

        quarter = cut // 2

        def quarters(v):
            return [v[..., p * quarter : (p + 1) * quarter] for p in range(2)]

        act = chips(act, 1, steps)
        grad_far = step(grad_far[0], take(grad_far[1]), 0)
        grad_near = steps_on(grad_near, 2, steps)
        grads = [total(grad_near[0], take(grad_near[1], *c_rows))]
        act = quarters(doubled(act, 1))
        acts = [(v, swap_chip(v, 0)) for v in act]
        grad_far = step(grad_far[0], take(grad_far[1]), 1)
        acts[0] = doubled(acts[0], 0)
        acts[0] = acts[0], swap_core(acts[0])
        grad_far = steps_on(grad_far, 2, steps)
        grads.append(total(grad_far[0], take(grad_far[1])))
        grad = lax.concatenate(grads, steps)
        hid, grad = lax.optimization_barrier((hid, grad))
        grad = chips((grad * gelu_parts(hid)[1]).astype(bf16), 1, steps)
        acts[1] = doubled(acts[1], 0)
        acts[1] = acts[1], swap_core(acts[1])
        acts[0] = acts[0][0], take(acts[0][1])
        acts[1] = acts[1][0], take(acts[1][1])

        sums = []
        for i, w in enumerate((w_out_own, w_out_other)):
            parts = [
                jnp.dot(flat(acts[p][i]), w[p * quarter : (p + 1) * quarter], preferred_element_type=f32)
                for p in range(2)
            ]
            sums.append((parts[0] + parts[1]).reshape(x_all.shape))
        mixed = jnp.where(core == 0, sums[0], sums[1]) + turn(jnp.where(core == 0, sums[1], sums[0]))
        mixed = mixed.astype(bf16)

        def halve(mixed, bit):
            blocks = mixed.shape[steps]
            mixed = mixed.reshape(mixed.shape[:steps] + (blocks // 2, 2) + mixed.shape[steps + 1 :])
            return (
                lax.index_in_dim(mixed, 0, steps + 1, False),
                reach(lax.index_in_dim(mixed, 1, steps + 1, False), 1 << bit),
            )

        def merged(flight):
            return (flight[0].astype(f32) + take(flight[1]).astype(f32)).astype(bf16)

        mixed = halve(mixed, 0)
        grad = quarters(doubled(grad, 1))
        grads = [(v, swap_chip(v, 0)) for v in grad]
        grad_w_out = jnp.zeros_like(w_out)
        for i, half in enumerate((own_half, other_half)):
            grad_w_out = weight_grad(flat(acts[0][i]), c_rows[i], half, 0, grad_w_out, False)
        grads[0] = lax.concatenate([grads[0][0], take(grads[0][1], grad_w_out)], 0)
        grads[0] = grads[0], swap_core(grads[0])
        for bit in range(1, col_bits):
            mixed = halve(merged(mixed), bit)
        for i, half in enumerate((own_half, other_half)):
            grad_w_out = weight_grad(flat(acts[1][i]), c_rows[i], half, 1, grad_w_out, False)
        grads[1] = lax.concatenate([grads[1][0], take(grads[1][1], grad_w_out)], 0)
        grads[1] = grads[1], swap_core(grads[1])
        grads[0] = grads[0][0], take(grads[0][1])
        grad_w_in = jnp.zeros_like(w_in)
        for p, i in ((0, 0), (0, 1), (1, 0)):
            grad_w_in = weight_grad(flat(grads[p][i]), x_rows[i], (own_half, other_half)[i], p, grad_w_in, True)
        mixed = flips(merged(mixed), first, 0).reshape(tokens, width)
        grad_w_in = weight_grad(flat(take(grads[1][1])), x_rows[1], other_half, 1, grad_w_in, True)
        return (mixed, grad_w_in, grad_w_out)

    return per_device


def solution(mesh):
    placed = (P("col", "row"), P("row", "col"), P("col", "row"), P("col", "row"))
    return jax.shard_map(
        make(mesh.shape["row"], mesh.shape["col"]),
        mesh=mesh,
        in_specs=placed,
        out_specs=(P("col", "row"), P("row", "col"), P("col", "row")),
        check_vma=False,
    )
```

time: 207 us -> 208 us (level)
  local copies, waits for them, and re-layouts: 9.58 us -> 23.8 us
  waiting for transfers between devices: 100 us -> 86.3 us
  starting transfers between devices: 28.3 us -> 31.3 us
    ppermute x5 -> x7, waiting for transfers between devices: 37.8 us -> 14.8 us  [reach(): return lax.ppermute(v, 'col', [(i, i ^ distance) for i in range(n_col)])]
    dynamic_slice x0 -> x2, local copies, waits for them, and re-layouts: none -> 14.9 us  [halves(): lax.dynamic_slice_in_dim(w, h * cut, cut, axis)]
    ppermute x14, waiting for transfers between devices: 59.4 us -> 71.5 us  [swap_chip(): lax.ppermute(v, 'row', [(i, i ^ 1 << orders[i & 1][step]) for i in range(...]
    convert_element_type x8 -> x4, other arithmetic: 6.47 us -> 0.75 us  [add_and_split(): total = (v.astype(f32) + got.astype(f32)).astype(bf16)]
    ppermute x8, waiting for transfers between devices: 3.01 us -> 0.02 us  [swap_core(): return lax.ppermute(v, 'row', [(i, i ^ 1) for i in range(n_row)])]
    ppermute x5 -> x7, starting transfers between devices: 10.4 us -> 13.2 us  [reach(): return lax.ppermute(v, 'col', [(i, i ^ distance) for i in range(n_col)])]
    concatenate x4, other arithmetic: 0.63 us -> 2.81 us  [doubled(): return lax.concatenate([flight[0], take(flight[1])], k)]
    unnamed x47 -> x37, local copies, waits for them, and re-layouts: 6.32 us -> 5.96 us
  transfers between devices with their start and end apart: 27 -> 29, of which waited for: 15 -> 15; matrix products, arithmetic and copies ran while one was open for 20% -> 32% of each run, Pallas kernels for 0% -> 0%
where the time goes in v2:
time: 208 us; the launch traced here: 207 us
  waiting for transfers between devices  86.3 us (41%)
  matrix products  47.6 us (23%)
  starting transfers between devices  31.3 us (15%)
  local copies, waits for them, and re-layouts  23.8 us (11%)
  other arithmetic  17.1 us (8%)
    ppermute x14, waiting for transfers between devices, swap_chip(): lax.ppermute(v, 'row', [(i, i ^ 1 << orders[i & 1][step]) for i in range(...  71.5 us
    ppermute x14, starting transfers between devices, swap_chip(): lax.ppermute(v, 'row', [(i, i ^ 1 << orders[i & 1][step]) for i in range(...  16.9 us
    dynamic_slice x2, local copies, waits for them, and re-layouts, halves(): lax.dynamic_slice_in_dim(w, h * cut, cut, axis)  14.9 us
    ppermute x7, waiting for transfers between devices, reach(): return lax.ppermute(v, 'col', [(i, i ^ distance) for i in range(n_col)])  14.8 us
    ppermute x7, starting transfers between devices, reach(): return lax.ppermute(v, 'col', [(i, i ^ distance) for i in range(n_col)])  13.2 us
    dot_general x4, matrix products, weight_grad(): out = jnp.dot(rows, piece, preferred_element_type=f32).astype(bf16)  11.7 us
    dot_general x2, matrix products, up(): jnp.dot(own, w_in_own, preferred_element_type=f32).astype(bf16)  7.77 us
    dot_general x4, matrix products, weight_grad(): lax.dot_general(piece, rows, (((0,), (0,)), ((), ())), preferred_element_...  7.48 us
  transfers between devices with their start and end apart: 29, of which 15 were waited for; matrix products, arithmetic and copies ran while one was open for 32% of the time, Pallas kernels for 0%

profile of v2, /device:TPU:0, one launch (start us, length us, event | category | flops | bytes accessed | tf_op | source)
XLA Modules:
  0.0 207.3 jit_solution(12393986846391061083)
XLA Ops:
  1.8 4.1 %collective-permute-start = (bf16[2,2,1,32,768]{4,3,2,1,0:T(8,128)(2,1)S(1)}, bf16[2,2,1,32,768]{4,3,2,1,0:T(8,128)(2,1)S(1)}, u32[]{:S(2)}, u32[]{:S(2)}) collective-permute-start(bf16[2,2,1,32,768]{4,3,2,1,0:T(8,128)(2,1)S(1)} %reverse_select_fusion.4), channel_id=1, source_target_pairs={{0,2},{1,3},{2,0},{3,1},{4,6},{5,7},{6,4},{7,5},{8,10},{9,11},{10,... | collective-permute-start | bytes 589832 | tf_op jit(solution)/shard_map/ppermute | solution.py:117
  8.7 8.4 %constant_dynamic-slice_fusion.2 = (bf16[768,3072]{1,0:T(8,128)(2,1)}, bf16[768,3072]{1,0:T(8,128)(2,1)}) fusion(bf16[768,6144]{1,0:T(8,128)(2,1)} %param.5, s32[]{:T(128)S(6)} %select_n.171, s32[]{:T(128)S(6)} %select_n.170), kind=kLoop, calls=%fused_computation.114 | loop fusion | bytes 18874376 | tf_op jit(solution)/shard_map/dynamic_slice | solution.py:83
  17.0 3.0 %collective-permute-done = bf16[2,2,1,32,768]{4,3,2,1,0:T(8,128)(2,1)S(1)} collective-permute-done((bf16[2,2,1,32,768]{4,3,2,1,0:T(8,128)(2,1)S(1)}, bf16[2,2,1,32,768]{4,3,2,1,0:T(8,128)(2,1)S(1)}, u32[]{:S(2)}, u32[]{:S(2)}) %collective-permute-start) | collective-permute-done | bytes 196640 | tf_op jit(solution)/shard_map/ppermute | solution.py:117
  20.1 5.9 %collective-permute-done.2 = bf16[2,2,1,32,1536]{4,3,2,1,0:T(8,128)(2,1)S(1)} collective-permute-done((bf16[2,2,1,32,1536]{4,3,2,1,0:T(8,128)(2,1)S(1)}, bf16[2,2,1,32,1536]{4,3,2,1,0:T(8,128)(2,1)S(1)}, u32[]{:S(2)}, u32[]{:S(2)}) %collective-permute-start.2) | collective-permute-done | bytes 393248 | tf_op jit(solution)/shard_map/ppermute | solution.py:117
  34.0 6.6 %constant_dynamic-slice_fusion = (bf16[3072,768]{1,0:T(8,128)(2,1)S(1)}, bf16[3072,768]{1,0:T(8,128)(2,1)}) fusion(bf16[6144,768]{1,0:T(8,128)(2,1)} %param.6, s32[]{:T(128)S(6)} %select_n.171, s32[]{:T(128)S(6)} %select_n.170), kind=kLoop, calls=%fused_computation.112 | loop fusion | bytes 18874376 | tf_op jit(solution)/shard_map/dynamic_slice | solution.py:83
  43.3 3.5 %collective-permute-start.11 = (bf16[2,2,1,32,768]{4,3,2,1,0:T(8,128)(2,1)S(1)}, bf16[2,2,1,32,768]{4,3,2,1,0:T(8,128)(2,1)S(1)}, u32[]{:S(2)}, u32[]{:S(2)}) collective-permute-start(bf16[2,2,1,32,768]{4,3,2,1,0:T(8,128)(2,1)S(1)} %reverse_select_fusion.2), channel_id=1, source_target_pairs={{0,3},{1,2},{2,1},{3,0},{4,7},{5,6},{6,5},{7,4},{8,11},{9,10},{10,... | collective-permute-start | bytes 589832 | tf_op jit(solution)/shard_map/ppermute | solution.py:117
  48.2 4.8 %add_convert_fusion.3 = bf16[256,3072]{1,0:T(8,128)(2,1)S(1)} fusion(bf16[256,3072]{1,0:T(8,128)(2,1)} %collective-permute-done.3, bf16[256,768]{1,0:T(8,128)(2,1)S(1)} %bitcast.140, bf16[768,3072]{1,0:T(8,128)(2,1)} %get-tuple-element.39), kind=kOutput, calls=%fused_computation.31 | convolution fusion | flops 1211891712 | bytes 8257536 | tf_op jit(solution)/shard_map/dot_general | solution.py:96
  54.6 3.0 %add_convert_fusion.2 = bf16[256,3072]{1,0:T(8,128)(2,1)S(1)} fusion(bf16[256,3072]{1,0:T(8,128)(2,1)} %collective-permute-done.6, bf16[256,768]{1,0:T(8,128)(2,1)S(1)} %bitcast.139, bf16[768,3072]{1,0:T(8,128)(2,1)S(1)} %bitcast.121), kind=kOutput, calls=%fused_computation.30 | convolution fusion | flops 1211891712 | bytes 8257536 | tf_op jit(solution)/shard_map/dot_general | solution.py:96
  58.6 3.0 %add_convert_fusion.1 = bf16[256,3072]{1,0:T(8,128)(2,1)S(1)} fusion(bf16[256,3072]{1,0:T(8,128)(2,1)} %collective-permute-done.5, bf16[256,768]{1,0:T(8,128)(2,1)S(1)} %bitcast.144, bf16[3072,768]{1,0:T(8,128)(2,1)S(1)} %bitcast.117), kind=kOutput, calls=%fused_computation.29 | convolution fusion | flops 1211891712 | bytes 8257536 | tf_op jit(solution)/shard_map/dot_general | solution.py:102
  65.3 8.2 %collective-permute-done.8 = bf16[128,3072]{1,0:T(8,128)(2,1)S(1)} collective-permute-done((bf16[128,3072]{1,0:T(8,128)(2,1)S(1)}, bf16[128,3072]{1,0:T(8,128)(2,1)S(1)}, u32[]{:S(2)}, u32[]{:S(2)}) %collective-permute-start.8) | collective-permute-done | bytes 786464 | tf_op jit(solution)/shard_map/ppermute | solution.py:43
  75.9 9.5 %collective-permute-done.7 = bf16[64,3072]{1,0:T(8,128)(2,1)S(1)} collective-permute-done((bf16[64,3072]{1,0:T(8,128)(2,1)S(1)}, bf16[64,3072]{1,0:T(8,128)(2,1)S(1)}, u32[]{:S(2)}, u32[]{:S(2)}) %collective-permute-start.7) | collective-permute-done | bytes 393248 | tf_op jit(solution)/shard_map/ppermute | solution.py:43
  96.0 12.5 %collective-permute-done.14 = bf16[64,3072]{1,0:T(8,128)(2,1)S(1)} collective-permute-done((bf16[64,3072]{1,0:T(8,128)(2,1)S(1)}, bf16[64,3072]{1,0:T(8,128)(2,1)S(1)}, u32[]{:S(2)}, u32[]{:S(2)}) %collective-permute-start.14) | collective-permute-done | bytes 393248 | tf_op jit(solution)/shard_map/ppermute | solution.py:43
  114.8 7.3 %collective-permute-done.17 = bf16[128,3072]{1,0:T(8,128)(2,1)S(1)} collective-permute-done((bf16[128,3072]{1,0:T(8,128)(2,1)S(1)}, bf16[128,3072]{1,0:T(8,128)(2,1)S(1)}, u32[]{:S(2)}, u32[]{:S(2)}) %collective-permute-start.17) | collective-permute-done | bytes 786464 | tf_op jit(solution)/shard_map/ppermute | solution.py:43
  124.0 10.8 %collective-permute-done.16 = bf16[1,2,4,32,1536]{4,3,2,1,0:T(8,128)(2,1)S(1)} collective-permute-done((bf16[1,2,4,32,1536]{4,3,2,1,0:T(8,128)(2,1)S(1)}, bf16[1,2,4,32,1536]{4,3,2,1,0:T(8,128)(2,1)S(1)}, u32[]{:S(2)}, u32[]{:S(2)}) %collective-permute-start.16) | collective-permute-done | bytes 786464 | tf_op jit(solution)/shard_map/ppermute | solution.py:43
  136.7 3.2 %fusion.11 = bf16[6144,768]{1,0:T(8,128)(2,1)S(1)} fusion(bf16[6144,768]{1,0:T(8,128)(2,1)S(1)} %broadcast_in_dim.6, s32[]{:T(128)S(6)} %select_n.170, bf16[512,1536]{1,0:T(8,128)(2,1)} %bitcast.24, bf16[512,768]{1,0:T(8,128)(2,1)} %bitcast.137), kind=kOutput, calls=%fused_computation.27 | convolution fusion | flops 1209139200 | bytes 4718596 | tf_op jit(solution)/shard_map/dot_general | solution.py:28
  148.4 2.9 %fusion.27 = f32[512,768]{1,0:T(8,128)S(1)} fusion(f32[512,768]{1,0:T(8,128)S(1)} %fusion.16, bf16[512,1536]{1,0:T(8,128)(2,1)} %bitcast.24, bf16[3072,768]{1,0:T(8,128)(2,1)S(1)} %bitcast.119), kind=kOutput, calls=%fused_computation.64 | convolution fusion | flops 1208352768 | bytes 7077888 | tf_op jit(solution)/shard_map/dot_general | solution.py:186
  154.2 3.4 %collective-permute-done.23 = bf16[1,1,4,32,3072]{4,3,2,1,0:T(8,128)(2,1)S(1)} collective-permute-done((bf16[1,1,4,32,3072]{4,3,2,1,0:T(8,128)(2,1)S(1)}, bf16[1,1,4,32,3072]{4,3,2,1,0:T(8,128)(2,1)S(1)}, u32[]{:S(2)}, u32[]{:S(2)}) %collective-permute-start.23) | collective-permute-done | bytes 786464 | tf_op jit(solution)/shard_map/ppermute | solution.py:43
  162.7 7.0 %collective-permute-done.24 = bf16[1,2,4,32,1536]{4,3,2,1,0:T(8,128)(2,1)S(1)} collective-permute-done((bf16[1,2,4,32,1536]{4,3,2,1,0:T(8,128)(2,1)S(1)}, bf16[1,2,4,32,1536]{4,3,2,1,0:T(8,128)(2,1)S(1)}, u32[]{:S(2)}, u32[]{:S(2)}) %collective-permute-start.24) | collective-permute-done | bytes 786464 | tf_op jit(solution)/shard_map/ppermute | solution.py:43
  173.9 4.2 %collective-permute-done.27 = bf16[1,2,4,32,1536]{4,3,2,1,0:T(8,128)(2,1)S(1)} collective-permute-done((bf16[1,2,4,32,1536]{4,3,2,1,0:T(8,128)(2,1)S(1)}, bf16[1,2,4,32,1536]{4,3,2,1,0:T(8,128)(2,1)S(1)}, u32[]{:S(2)}, u32[]{:S(2)}) %collective-permute-start.27) | collective-permute-done | bytes 786464 | tf_op jit(solution)/shard_map/ppermute | solution.py:43
  180.2 2.9 %collective-permute-start.25 = (bf16[2,2,1,32,768]{4,3,2,1,0:T(8,128)(2,1)}, bf16[2,2,1,32,768]{4,3,2,1,0:T(8,128)(2,1)}, u32[]{:S(2)}, u32[]{:S(2)}) collective-permute-start(bf16[2,2,1,32,768]{4,3,2,1,0:T(8,128)(2,1)} %slice_bitcast_fusion), channel_id=1, source_target_pairs={{0,2},{1,3},{2,0},{3,1},{4,6},{5,7},{6,4},{7,5},{8,10},{9,11},{10,... | collective-permute-start | bytes 589832 | tf_op jit(solution)/shard_map/ppermute | solution.py:117
  184.3 3.1 %fusion.7 = bf16[768,6144]{1,0:T(8,128)(2,1)S(1)} fusion(bf16[768,6144]{1,0:T(8,128)(2,1)S(1)} %broadcast_in_dim.7, s32[]{:T(128)S(6)} %select_n.170, bf16[768,512]{0,1:T(8,128)(2,1)} %bitcast.133, bf16[512,1536]{1,0:T(8,128)(2,1)} %bitcast.41), kind=kOutput, calls=%fused_computation.19 | convolution fusion | flops 1209139200 | bytes 4718596 | tf_op jit(solution)/shard_map/dot_general | solution.py:26
  187.5 5.8 %collective-permute-done.25 = bf16[2,2,1,32,768]{4,3,2,1,0:T(8,128)(2,1)} collective-permute-done((bf16[2,2,1,32,768]{4,3,2,1,0:T(8,128)(2,1)}, bf16[2,2,1,32,768]{4,3,2,1,0:T(8,128)(2,1)}, u32[]{:S(2)}, u32[]{:S(2)}) %collective-permute-start.25) | collective-permute-done | bytes 196640 | tf_op jit(solution)/shard_map/ppermute | solution.py:117
  195.0 2.9 %fusion.6 = bf16[768,6144]{1,0:T(8,128)(2,1)S(1)} fusion(bf16[768,6144]{1,0:T(8,128)(2,1)S(1)} %fusion.7, s32[]{:T(128)S(6)} %select_n.171, bf16[768,512]{0,1:T(8,128)(2,1)S(1)} %bitcast.131, bf16[512,1536]{1,0:T(8,128)(2,1)} %bitcast.42), kind=kOutput, calls=%fused_computation.17 | convolution fusion | flops 1209139200 | bytes 4718596 | tf_op jit(solution)/shard_map/dot_general | solution.py:26
  203.6 3.7 %copy-done.1 = bf16[768,6144]{1,0:T(8,128)(2,1)} copy-done((bf16[768,6144]{1,0:T(8,128)(2,1)}, bf16[768,6144]{1,0:T(8,128)(2,1)S(1)}, u32[]{:S(2)}) %copy-start.1) | copy-done | bytes 9437208
  (148 shorter events, 76.2 us)
Async XLA Ops:
  1.8 18.3 %collective-permute-start = (bf16[2,2,1,32,768]{4,3,2,1,0:T(8,128)(2,1)S(1)}, bf16[2,2,1,32,768]{4,3,2,1,0:T(8,128)(2,1)S(1)}, u32[]{:S(2)}, u32[]{:S(2)}) collective-permute-start(bf16[2,2,1,32,768]{4,3,2,1,0:T(8,128)(2,1)S(1)} %reverse_select_fusion.4), channel_id=1, source_target_pairs={{0,2},{1,3},{2,0},{3,1},{4,6},{5,7},{6,4},{7,5},{8,10},{9,11},{10,... | collective-permute-start | bytes 589832 | tf_op jit(solution)/shard_map/ppermute | solution.py:117
  5.9 14.2 %collective-permute-start.1 = (bf16[2,2,1,32,768]{4,3,2,1,0:T(8,128)(2,1)S(1)}, bf16[2,2,1,32,768]{4,3,2,1,0:T(8,128)(2,1)S(1)}, u32[]{:S(2)}, u32[]{:S(2)}) collective-permute-start(bf16[2,2,1,32,768]{4,3,2,1,0:T(8,128)(2,1)S(1)} %reverse_select_fusion.4), channel_id=1, source_target_pairs={{0,3},{1,2},{2,1},{3,0},{4,7},{5,6},{6,5},{7,4},{8,11},{9,10},{10,... | collective-permute-start | bytes 589832 | tf_op jit(solution)/shard_map/ppermute | solution.py:117
  8.4 17.6 %collective-permute-start.2 = (bf16[2,2,1,32,1536]{4,3,2,1,0:T(8,128)(2,1)S(1)}, bf16[2,2,1,32,1536]{4,3,2,1,0:T(8,128)(2,1)S(1)}, u32[]{:S(2)}, u32[]{:S(2)}) collective-permute-start(bf16[2,2,1,32,1536]{4,3,2,1,0:T(8,128)(2,1)S(1)} %pad_maximum_fusion.10), channel_id=1, source_target_pairs={{0,1},{1,0},{2,3},{3,2},{4,5},{5,4},{6,7},{7,6},{8,9},{9,8},{10,11... | collective-permute-start | bytes 1179656 | tf_op jit(solution)/shard_map/ppermute | solution.py:117
  31.0 17.2 %collective-permute-start.6 = (bf16[256,3072]{1,0:T(8,128)(2,1)}, bf16[256,3072]{1,0:T(8,128)(2,1)}, u32[]{:S(2)}, u32[]{:S(2)}) collective-permute-start(bf16[256,3072]{1,0:T(8,128)(2,1)} %convolution_convert_fusion.4), channel_id=1, source_target_pairs={{0,4},{4,0},{8,12},{12,8},{16,20},{20,16},{24,28},{28,24},{1,5},{5... | collective-permute-start | bytes 4718600 | tf_op jit(solution)/shard_map/ppermute | solution.py:40
  33.5 14.7 %collective-permute-start.3 = (bf16[256,3072]{1,0:T(8,128)(2,1)}, bf16[256,3072]{1,0:T(8,128)(2,1)}, u32[]{:S(2)}, u32[]{:S(2)}) collective-permute-start(bf16[256,3072]{1,0:T(8,128)(2,1)} %convolution_convert_fusion.6), channel_id=1, source_target_pairs={{0,4},{4,0},{8,12},{12,8},{16,20},{20,16},{24,28},{28,24},{1,5},{5... | collective-permute-start | bytes 4718600 | tf_op jit(solution)/shard_map/ppermute | solution.py:40
  43.3 15.3 %collective-permute-start.5 = (bf16[256,3072]{1,0:T(8,128)(2,1)}, bf16[256,3072]{1,0:T(8,128)(2,1)}, u32[]{:S(2)}, u32[]{:S(2)}) collective-permute-start(bf16[256,3072]{1,0:T(8,128)(2,1)} %convolution_convert_fusion.5), channel_id=1, source_target_pairs={{0,4},{4,0},{8,12},{12,8},{16,20},{20,16},{24,28},{28,24},{1,5},{5... | collective-permute-start | bytes 4718600 | tf_op jit(solution)/shard_map/ppermute | solution.py:40
  43.3 42.2 %collective-permute-start.11 = (bf16[2,2,1,32,768]{4,3,2,1,0:T(8,128)(2,1)S(1)}, bf16[2,2,1,32,768]{4,3,2,1,0:T(8,128)(2,1)S(1)}, u32[]{:S(2)}, u32[]{:S(2)}) collective-permute-start(bf16[2,2,1,32,768]{4,3,2,1,0:T(8,128)(2,1)S(1)} %reverse_select_fusion.2), channel_id=1, source_target_pairs={{0,3},{1,2},{2,1},{3,0},{4,7},{5,6},{6,5},{7,4},{8,11},{9,10},{10,... | collective-permute-start | bytes 589832 | tf_op jit(solution)/shard_map/ppermute | solution.py:117
  46.8 38.7 %collective-permute-start.12 = (bf16[2,2,1,32,768]{4,3,2,1,0:T(8,128)(2,1)S(1)}, bf16[2,2,1,32,768]{4,3,2,1,0:T(8,128)(2,1)S(1)}, u32[]{:S(2)}, u32[]{:S(2)}) collective-permute-start(bf16[2,2,1,32,768]{4,3,2,1,0:T(8,128)(2,1)S(1)} %reverse_select_fusion.2), channel_id=1, source_target_pairs={{0,2},{1,3},{2,0},{3,1},{4,6},{5,7},{6,4},{7,5},{8,10},{9,11},{10,... | collective-permute-start | bytes 589832 | tf_op jit(solution)/shard_map/ppermute | solution.py:117
  53.0 12.1 %collective-permute-start.4 = (bf16[128,3072]{1,0:T(8,128)(2,1)S(1)}, bf16[128,3072]{1,0:T(8,128)(2,1)S(1)}, u32[]{:S(2)}, u32[]{:S(2)}) collective-permute-start(bf16[128,3072]{1,0:T(8,128)(2,1)S(1)} %slice.121), channel_id=1, source_target_pairs={{0,8},{4,20},{8,0},{12,28},{16,24},{20,4},{24,16},{28,12},{1,9},{5... | collective-permute-start | bytes 2359304 | tf_op jit(solution)/shard_map/ppermute | solution.py:43
  57.7 15.8 %collective-permute-start.8 = (bf16[128,3072]{1,0:T(8,128)(2,1)S(1)}, bf16[128,3072]{1,0:T(8,128)(2,1)S(1)}, u32[]{:S(2)}, u32[]{:S(2)}) collective-permute-start(bf16[128,3072]{1,0:T(8,128)(2,1)S(1)} %slice.124), channel_id=1, source_target_pairs={{0,8},{4,20},{8,0},{12,28},{16,24},{20,4},{24,16},{28,12},{1,9},{5... | collective-permute-start | bytes 2359304 | tf_op jit(solution)/shard_map/ppermute | solution.py:43
  61.7 26.6 %collective-permute-start.10 = (bf16[128,3072]{1,0:T(8,128)(2,1)S(1)}, bf16[128,3072]{1,0:T(8,128)(2,1)S(1)}, u32[]{:S(2)}, u32[]{:S(2)}) collective-permute-start(bf16[128,3072]{1,0:T(8,128)(2,1)S(1)} %slice.128), channel_id=1, source_target_pairs={{0,8},{4,20},{8,0},{12,28},{16,24},{20,4},{24,16},{28,12},{1,9},{5... | collective-permute-start | bytes 2359304 | tf_op jit(solution)/shard_map/ppermute | solution.py:43
  75.4 14.3 %collective-permute-start.9 = (bf16[64,3072]{1,0:T(8,128)(2,1)S(1)}, bf16[64,3072]{1,0:T(8,128)(2,1)S(1)}, u32[]{:S(2)}, u32[]{:S(2)}) collective-permute-start(bf16[64,3072]{1,0:T(8,128)(2,1)S(1)} %slice.127), channel_id=1, source_target_pairs={{0,16},{4,12},{8,24},{12,4},{16,0},{20,28},{24,8},{28,20},{1,17},{... | collective-permute-start | bytes 1179656 | tf_op jit(solution)/shard_map/ppermute | solution.py:43
  92.3 16.3 %collective-permute-start.13 = (bf16[1,1,4,32,3072]{4,3,2,1,0:T(8,128)(2,1)S(1)}, bf16[1,1,4,32,3072]{4,3,2,1,0:T(8,128)(2,1)S(1)}, u32[]{:S(2)}, u32[]{:S(2)}) collective-permute-start(bf16[1,1,4,32,3072]{4,3,2,1,0:T(8,128)(2,1)S(1)} %get-tuple-element.82), channel_id=1, source_target_pairs={{0,16},{4,12},{8,24},{12,4},{16,0},{20,28},{24,8},{28,20},{1,17},{... | collective-permute-start | bytes 2359304 | tf_op jit(solution)/shard_map/ppermute | solution.py:43
  94.1 14.5 %collective-permute-start.14 = (bf16[64,3072]{1,0:T(8,128)(2,1)S(1)}, bf16[64,3072]{1,0:T(8,128)(2,1)S(1)}, u32[]{:S(2)}, u32[]{:S(2)}) collective-permute-start(bf16[64,3072]{1,0:T(8,128)(2,1)S(1)} %slice.130), channel_id=1, source_target_pairs={{0,16},{4,12},{8,24},{12,4},{16,0},{20,28},{24,8},{28,20},{1,17},{... | collective-permute-start | bytes 1179656 | tf_op jit(solution)/shard_map/ppermute | solution.py:43
  110.1 12.1 %collective-permute-start.17 = (bf16[128,3072]{1,0:T(8,128)(2,1)S(1)}, bf16[128,3072]{1,0:T(8,128)(2,1)S(1)}, u32[]{:S(2)}, u32[]{:S(2)}) collective-permute-start(bf16[128,3072]{1,0:T(8,128)(2,1)S(1)} %slice.133), channel_id=1, source_target_pairs={{0,8},{4,20},{8,0},{12,28},{16,24},{20,4},{24,16},{28,12},{1,9},{5... | collective-permute-start | bytes 2359304 | tf_op jit(solution)/shard_map/ppermute | solution.py:43
  111.8 23.0 %collective-permute-start.16 = (bf16[1,2,4,32,1536]{4,3,2,1,0:T(8,128)(2,1)S(1)}, bf16[1,2,4,32,1536]{4,3,2,1,0:T(8,128)(2,1)S(1)}, u32[]{:S(2)}, u32[]{:S(2)}) collective-permute-start(bf16[1,2,4,32,1536]{4,3,2,1,0:T(8,128)(2,1)S(1)} %get-tuple-element.83), channel_id=1, source_target_pairs={{0,8},{4,20},{8,0},{12,28},{16,24},{20,4},{24,16},{28,12},{1,9},{5... | collective-permute-start | bytes 2359304 | tf_op jit(solution)/shard_map/ppermute | solution.py:43
  113.3 30.0 %collective-permute-start.18 = (bf16[1,2,4,32,1536]{4,3,2,1,0:T(8,128)(2,1)S(1)}, bf16[1,2,4,32,1536]{4,3,2,1,0:T(8,128)(2,1)}, u32[]{:S(2)}, u32[]{:S(2)}) collective-permute-start(bf16[1,2,4,32,1536]{4,3,2,1,0:T(8,128)(2,1)S(1)} %get-tuple-element.84), channel_id=1, source_target_pairs={{0,8},{4,20},{8,0},{12,28},{16,24},{20,4},{24,16},{28,12},{1,9},{5... | collective-permute-start | bytes 2359304 | tf_op jit(solution)/shard_map/ppermute | solution.py:43
  122.4 17.5 %collective-permute-start.19 = (bf16[64,3072]{1,0:T(8,128)(2,1)S(1)}, bf16[64,3072]{1,0:T(8,128)(2,1)}, u32[]{:S(2)}, u32[]{:S(2)}) collective-permute-start(bf16[64,3072]{1,0:T(8,128)(2,1)S(1)} %slice.135), channel_id=1, source_target_pairs={{0,16},{4,12},{8,24},{12,4},{16,0},{20,28},{24,8},{28,20},{1,17},{... | collective-permute-start | bytes 1179656 | tf_op jit(solution)/shard_map/ppermute | solution.py:43
  136.1 15.3 %collective-permute-start.20 = (bf16[2,2,4,32,1536]{4,3,2,1,0:T(8,128)(2,1)}, bf16[2,2,4,32,1536]{4,3,2,1,0:T(8,128)(2,1)S(1)}, u32[]{:S(2)}, u32[]{:S(2)}) collective-permute-start(bf16[2,2,4,32,1536]{4,3,2,1,0:T(8,128)(2,1)} %pad_maximum_fusion.1), channel_id=1, source_target_pairs={{0,4},{4,0},{8,12},{12,8},{16,20},{20,16},{24,28},{28,24},{1,5},{5... | collective-permute-start | bytes 4718600 | tf_op jit(solution)/shard_map/ppermute | solution.py:40
  145.5 12.1 %collective-permute-start.23 = (bf16[1,1,4,32,3072]{4,3,2,1,0:T(8,128)(2,1)S(1)}, bf16[1,1,4,32,3072]{4,3,2,1,0:T(8,128)(2,1)S(1)}, u32[]{:S(2)}, u32[]{:S(2)}) collective-permute-start(bf16[1,1,4,32,3072]{4,3,2,1,0:T(8,128)(2,1)S(1)} %fusion.25), channel_id=1, source_target_pairs={{0,16},{4,12},{8,24},{12,4},{16,0},{20,28},{24,8},{28,20},{1,17},{... | collective-permute-start | bytes 2359304 | tf_op jit(solution)/shard_map/ppermute | solution.py:43
  162.2 16.0 %collective-permute-start.27 = (bf16[1,2,4,32,1536]{4,3,2,1,0:T(8,128)(2,1)S(1)}, bf16[1,2,4,32,1536]{4,3,2,1,0:T(8,128)(2,1)S(1)}, u32[]{:S(2)}, u32[]{:S(2)}) collective-permute-start(bf16[1,2,4,32,1536]{4,3,2,1,0:T(8,128)(2,1)S(1)} %get-tuple-element.79), channel_id=1, source_target_pairs={{0,8},{4,20},{8,0},{12,28},{16,24},{20,4},{24,16},{28,12},{1,9},{5... | collective-permute-start | bytes 2359304 | tf_op jit(solution)/shard_map/ppermute | solution.py:43
  171.0 16.5 %collective-permute-start.26 = (bf16[2,2,4,32,1536]{4,3,2,1,0:T(8,128)(2,1)}, bf16[2,2,4,32,1536]{4,3,2,1,0:T(8,128)(2,1)}, u32[]{:S(2)}, u32[]{:S(2)}) collective-permute-start(bf16[2,2,4,32,1536]{4,3,2,1,0:T(8,128)(2,1)} %pad_maximum_fusion.4), channel_id=1, source_target_pairs={{0,4},{4,0},{8,12},{12,8},{16,20},{20,16},{24,28},{28,24},{1,5},{5... | collective-permute-start | bytes 4718600 | tf_op jit(solution)/shard_map/ppermute | solution.py:40
  179.4 15.6 %collective-permute-start.28 = (bf16[2,2,4,32,1536]{4,3,2,1,0:T(8,128)(2,1)}, bf16[2,2,4,32,1536]{4,3,2,1,0:T(8,128)(2,1)}, u32[]{:S(2)}, u32[]{:S(2)}) collective-permute-start(bf16[2,2,4,32,1536]{4,3,2,1,0:T(8,128)(2,1)} %pad_maximum_fusion.5), channel_id=1, source_target_pairs={{0,4},{4,0},{8,12},{12,8},{16,20},{20,16},{24,28},{28,24},{1,5},{5... | collective-permute-start | bytes 4718600 | tf_op jit(solution)/shard_map/ppermute | solution.py:40
  180.2 13.0 %collective-permute-start.25 = (bf16[2,2,1,32,768]{4,3,2,1,0:T(8,128)(2,1)}, bf16[2,2,1,32,768]{4,3,2,1,0:T(8,128)(2,1)}, u32[]{:S(2)}, u32[]{:S(2)}) collective-permute-start(bf16[2,2,1,32,768]{4,3,2,1,0:T(8,128)(2,1)} %slice_bitcast_fusion), channel_id=1, source_target_pairs={{0,2},{1,3},{2,0},{3,1},{4,6},{5,7},{6,4},{7,5},{8,10},{9,11},{10,... | collective-permute-start | bytes 589832 | tf_op jit(solution)/shard_map/ppermute | solution.py:117
  (22 other events, 196.8 us)
